TPU v7x, 32 devices: a whole 2x2x4 slice. The times are simulated.
32 devices in a mesh: dp: 4 (over y, x), seq: 8 (over z, core).
Axes of the slice: x: 2, y: 2, z: 4, core: 2. Of those that a mesh axis runs over, the one named last changes fastest.
Arguments:
- frames: float32 [16, 2048, 256], P('dp', 'seq'), may hold values from -6 to 6
- flow_embed: float32 [16, 1024], P('dp'), may hold values from -6 to 6
- lengths: int32 [16], P('dp'), may hold values from 256 to 2048, as said below
- cotangent: float32 [16, 1024, 256], P('dp', 'seq'), may hold values from -6 to 6
- conv_one: bfloat16 [2, 3, 256, 256], replicated, may hold values from -0.21875 to 0.21875
- conv_two: bfloat16 [2, 3, 256, 256], replicated, may hold values from -0.21875 to 0.21875
- res_weight: bfloat16 [2, 256, 256], replicated, may hold values from -0.375 to 0.375
- norm_gain: bfloat16 [2, 2, 256], replicated, may hold values from 0.25 to 1.75
- norm_bias: bfloat16 [2, 2, 256], replicated, may hold values from -3 to 3
- time_weight: bfloat16 [2, 1024, 256], replicated, may hold values from -0.1875 to 0.1875
- time_bias: bfloat16 [2, 256], replicated, may hold values from -3 to 3
- layer_gain: bfloat16 [2, 2, 256], replicated, may hold values from 0.25 to 1.75
- layer_bias: bfloat16 [2, 2, 256], replicated, may hold values from -1.75 to 1.75
- qkv_weight: bfloat16 [2, 256, 384], replicated, may hold values from -0.375 to 0.375
- out_weight: bfloat16 [2, 128, 256], replicated, may hold values from -1.5 to 1.5
- out_bias: bfloat16 [2, 256], replicated, may hold values from -1.75 to 1.75
- up_weight: bfloat16 [2, 256, 1024], replicated, may hold values from -0.375 to 0.375
- up_bias: bfloat16 [2, 1024], replicated, may hold values from -3 to 3
- snake_alpha: bfloat16 [2, 1024], replicated, may hold values from -1 to 1
- snake_beta: bfloat16 [2, 1024], replicated, may hold values from -0.5 to 0.5
- down_weight: bfloat16 [2, 1024, 256], replicated, may hold values from -0.1875 to 0.1875
- down_bias: bfloat16 [2, 256], replicated, may hold values from -1.75 to 1.75
- shrink_weight: bfloat16 [3, 256, 256], replicated, may hold values from -0.21875 to 0.21875
- shrink_bias: bfloat16 [256], replicated, may hold values from -1.75 to 1.75
Outputs:
- output: float32 [16, 1024, 256], P('dp', 'seq')
- input_grad: float32 [16, 2048, 256], P('dp', 'seq')
- grad_conv_one: float32 [2, 3, 256, 256], replicated
- grad_conv_two: float32 [2, 3, 256, 256], replicated
- grad_res_weight: float32 [2, 256, 256], replicated
- grad_norm_gain: float32 [2, 2, 256], replicated
- grad_norm_bias: float32 [2, 2, 256], replicated
- grad_time_weight: float32 [2, 1024, 256], replicated
- grad_time_bias: float32 [2, 256], replicated
- grad_layer_gain: float32 [2, 2, 256], replicated
- grad_layer_bias: float32 [2, 2, 256], replicated
- grad_qkv_weight: float32 [2, 256, 384], replicated
- grad_out_weight: float32 [2, 128, 256], replicated
- grad_out_bias: float32 [2, 256], replicated
- grad_up_weight: float32 [2, 256, 1024], replicated
- grad_up_bias: float32 [2, 1024], replicated
- grad_snake_alpha: float32 [2, 1024], replicated
- grad_snake_beta: float32 [2, 1024], replicated
- grad_down_weight: float32 [2, 1024, 256], replicated
- grad_down_bias: float32 [2, 256], replicated
- grad_shrink_weight: float32 [3, 256, 256], replicated
- grad_shrink_bias: float32 [256], replicated
Inputs may be any that keep to these rules, and one draw needn't show every extreme that they name: `lengths`: of the two utterances 2 i and 2 i + 1, one has exactly 2048 frames.
All inputs are finite; a program needn't handle non-finite values.
Results may differ from a plain program's by a relative error of at most 0.0003.
Values sent between devices are 32-bit elements; how exact they have to be, the bound alone decides.
A program may use at most 640 MiB of HBM per device.

v0:
```python
import math

import jax
import jax.numpy as jnp
from jax import lax
from jax.sharding import PartitionSpec as P

HEADS = 2
GROUPS = 8


precise = lax.Precision.HIGHEST
epsilon = 1e-05


def with_halo(value, sides, width):
    for axis, dim in sides:
        count, length = (lax.axis_size(axis), value.shape[dim])
        up = [(i, (i + 1) % count) for i in range(count - 1)]
        down = [(j, i) for i, j in up]
        last = lax.slice_in_dim(value, length - width, length, axis=dim)
        first = lax.slice_in_dim(value, 0, width, axis=dim)
        before = lax.ppermute(last, axis, up)
        after = lax.ppermute(first, axis, down)
        value = jnp.concatenate([before, value, after], axis=dim)
    return value


def shifted(value, axis, by):
    count = lax.axis_size(axis)
    pairs = [(i, i + by) for i in range(count) if 0 <= i + by < count]
    return lax.ppermute(value, axis, pairs)


def mish_curve(value_in):
    return value_in * jnp.tanh(jax.nn.softplus(value_in))


def conv_piece(padded, weight):
    frames_out = padded.shape[1] - 2
    summed = jnp.einsum("ufc,cd->ufd", padded[:, :frames_out], weight[0], precision=precise)
    summed = summed + jnp.einsum(
        "ufc,cd->ufd", padded[:, 1 : frames_out + 1], weight[1], precision=precise
    )
    return summed + jnp.einsum("ufc,cd->ufd", padded[:, 2:], weight[2], precision=precise)


def shrink_piece(padded, weight, bias_vec):
    span_len = padded.shape[1] - 1
    summed = jnp.einsum("ufc,cd->ufd", padded[:, 0:span_len:2], weight[0], precision=precise)
    summed = summed + jnp.einsum(
        "ufc,cd->ufd", padded[:, 1:span_len:2], weight[1], precision=precise
    )
    summed = summed + jnp.einsum(
        "ufc,cd->ufd", padded[:, 2 : span_len + 1 : 2], weight[2], precision=precise
    )
    return summed + bias_vec


def group_sums(conv_out, mask_row):
    utterances, frames_in, channels = conv_out.shape
    masked = conv_out * mask_row[:, :, None]
    shape_new = (utterances, frames_in, GROUPS, channels // GROUPS)
    first_sum = jnp.sum(masked.reshape(shape_new), axis=(1, 3))
    second_sum = jnp.sum((masked * conv_out).reshape(shape_new), axis=(1, 3))
    return (first_sum, second_sum)


def group_apply(conv_out, first_sum, second_sum, counts, gain_vec, bias_vec, mask_row):
    group_width = conv_out.shape[2] // GROUPS
    mean_val = first_sum / counts[:, None]
    var_val = second_sum / counts[:, None] - mean_val * mean_val
    scale_val = lax.rsqrt(var_val + epsilon)
    mean_full = jnp.repeat(mean_val, group_width, axis=1)[:, None, :]
    scale_full = jnp.repeat(scale_val, group_width, axis=1)[:, None, :]
    normed = (conv_out - mean_full) * scale_full * gain_vec + bias_vec
    return mish_curve(normed) * mask_row[:, :, None]


def time_piece(embedding, weight, bias_vec):
    return jnp.dot(mish_curve(embedding), weight, precision=precise) + bias_vec


def layer_norm(value_in, gain_vec, bias_vec):
    mean_val = jnp.mean(value_in, axis=-1, keepdims=True)
    centered = value_in - mean_val
    var_val = jnp.mean(centered * centered, axis=-1, keepdims=True)
    return centered * lax.rsqrt(var_val + epsilon) * gain_vec + bias_vec


def attend_in(value_in, gain_vec, bias_vec, qkv_weight):
    normed = layer_norm(value_in, gain_vec, bias_vec)
    packed = jnp.einsum("ufc,ce->ufe", normed, qkv_weight, precision=precise)
    inner_dim = packed.shape[2] // 3
    return (
        packed[:, :, :inner_dim],
        packed[:, :, inner_dim : 2 * inner_dim],
        packed[:, :, 2 * inner_dim :],
    )


def attend_out(value_in, queries, key_full, value_full, key_mask, later_weights):
    (
        out_weight,
        out_bias,
        gain_vec,
        bias_vec,
        up_weight,
        up_bias,
        snake_alpha,
        snake_beta,
        down_weight,
        down_bias,
    ) = later_weights
    utterances, frames_in, inner_dim = queries.shape
    head_dim = inner_dim // HEADS
    key_count = key_full.shape[1]
    query_heads = queries.reshape(utterances, frames_in, HEADS, head_dim)
    key_heads = key_full.reshape(utterances, key_count, HEADS, head_dim)
    value_heads = value_full.reshape(utterances, key_count, HEADS, head_dim)
    scores = jnp.einsum("uqhd,ukhd->uhqk", query_heads, key_heads, precision=precise) / math.sqrt(
        head_dim
    )
    scores = jnp.where(key_mask[:, None, None, :] > 0.5, scores, -1e30)
    scores = scores - jnp.max(scores, axis=3, keepdims=True)
    raised = jnp.exp(scores)
    weights_soft = raised / jnp.sum(raised, axis=3, keepdims=True)
    attended = jnp.einsum("uhqk,ukhd->uqhd", weights_soft, value_heads, precision=precise)
    attended = attended.reshape(utterances, frames_in, inner_dim)
    current = (
        value_in + jnp.einsum("ufe,ec->ufc", attended, out_weight, precision=precise) + out_bias
    )
    normed = layer_norm(current, gain_vec, bias_vec)
    raised_up = jnp.einsum("ufc,ce->ufe", normed, up_weight, precision=precise) + up_bias
    snake_out = raised_up + jnp.sin(raised_up * jnp.exp(snake_alpha)) ** 2 / (
        jnp.exp(snake_beta) + 1e-09
    )
    return (
        current + jnp.einsum("ufe,ec->ufc", snake_out, down_weight, precision=precise) + down_bias
    )


def layer_weights(stacked, layer_index):
    (
        conv_one,
        conv_two,
        res_weight,
        norm_gain,
        norm_bias,
        time_weight,
        time_bias,
        layer_gain,
        layer_bias,
        qkv_weight,
        out_weight,
        out_bias,
        up_weight,
        up_bias,
        snake_alpha,
        snake_beta,
        down_weight,
        down_bias,
    ) = stacked
    resnet_part = (
        conv_one[layer_index],
        conv_two[layer_index],
        res_weight[layer_index],
        norm_gain[layer_index],
        norm_bias[layer_index],
        time_weight[layer_index],
        time_bias[layer_index],
    )
    first_part = (layer_gain[layer_index, 0], layer_bias[layer_index, 0], qkv_weight[layer_index])
    later_part = (
        out_weight[layer_index],
        out_bias[layer_index],
        layer_gain[layer_index, 1],
        layer_bias[layer_index, 1],
        up_weight[layer_index],
        up_bias[layer_index],
        snake_alpha[layer_index],
        snake_beta[layer_index],
        down_weight[layer_index],
        down_bias[layer_index],
    )
    return (resnet_part, first_part, later_part)


def layer_grads(resnet_grads, first_grads, later_grads):
    gains = jnp.stack([first_grads[0], later_grads[2]])
    biases = jnp.stack([first_grads[1], later_grads[3]])
    return (
        resnet_grads
        + (gains, biases, first_grads[2], later_grads[0], later_grads[1])
        + later_grads[4:]
    )


def flatten_all(arrays):
    return jnp.concatenate([array_in.reshape(-1) for array_in in arrays])


def unflatten_all(flat, shapes):
    pieces = []
    offset_at = 0
    for shape_in in shapes:
        size_in = math.prod(shape_in)
        pieces.append(flat[offset_at : offset_at + size_in].reshape(shape_in))
        offset_at = offset_at + size_in
    return pieces


def frame_halo(value_in):
    return with_halo(value_in, (("seq", 1),), 1)


def rim_return(grad_padded):
    rim_rows = jnp.concatenate([grad_padded[:, :1], grad_padded[:, -1:]], axis=1)
    arrived = with_halo(rim_rows, (("seq", 1),), 1)
    inner_rows = grad_padded[:, 1:-1]
    inner_rows = inner_rows.at[:, 0].add(arrived[:, 0])
    return inner_rows.at[:, -1].add(arrived[:, 3])


def group_total(conv_out, mask_row):
    first_sum, second_sum = group_sums(conv_out, mask_row)
    return lax.psum((first_sum, second_sum), "seq")


def group_return(conv_out, mask_row, grad_first, grad_second):
    grad_first, grad_second = lax.psum((grad_first, grad_second), "seq")

    def sums_local(conv_in):
        return group_sums(conv_in, mask_row)

    pull_back = jax.vjp(sums_local, conv_out)[1]
    return pull_back((grad_first, grad_second))[0]


def resnet_forward(inputs, mask_row, counts, embedding, weights):
    conv_first, conv_second, res_weight, norm_gain, norm_bias, time_weight, time_bias = weights
    column = mask_row[:, :, None]
    masked = inputs * column
    padded_one = frame_halo(masked)
    first_conv = conv_piece(padded_one, conv_first)
    sums_one = group_total(first_conv, mask_row)
    hidden = group_apply(
        first_conv, sums_one[0], sums_one[1], counts, norm_gain[0], norm_bias[0], mask_row
    )
    hidden = hidden + time_piece(embedding, time_weight, time_bias)[:, None, :]
    padded_two = frame_halo(hidden * column)
    second = conv_piece(padded_two, conv_second)
    sums_two = group_total(second, mask_row)
    result = group_apply(
        second, sums_two[0], sums_two[1], counts, norm_gain[1], norm_bias[1], mask_row
    )
    result = result + jnp.einsum("ufc,cd->ufd", masked, res_weight, precision=precise)
    return (result, (masked, padded_one, first_conv, sums_one, padded_two, second, sums_two))


def resnet_backward(grad_out, saved, mask_row, counts, embedding, weights):
    conv_first, conv_second, res_weight, norm_gain, norm_bias, time_weight, time_bias = weights
    masked, padded_one, first_conv, sums_one, padded_two, second, sums_two = saved
    column = mask_row[:, :, None]

    def norm_local(conv_out, first_sum, second_sum, gain_vec, bias_vec):
        return group_apply(conv_out, first_sum, second_sum, counts, gain_vec, bias_vec, mask_row)

    pull_two = jax.vjp(norm_local, second, sums_two[0], sums_two[1], norm_gain[1], norm_bias[1])[1]
    grad_second, grad_first_sum, grad_second_sum, gain_grad_two, bias_grad_two = pull_two(grad_out)
    grad_second = grad_second + group_return(second, mask_row, grad_first_sum, grad_second_sum)
    grad_res = jnp.einsum("ufc,ufd->cd", masked, grad_out, precision=precise)
    grad_masked = jnp.einsum("ufd,cd->ufc", grad_out, res_weight, precision=precise)
    pull_conv = jax.vjp(conv_piece, padded_two, conv_second)[1]
    grad_padded, grad_conv_second = pull_conv(grad_second)
    grad_hidden = rim_return(grad_padded) * column

    def time_local(weight, bias_vec):
        return time_piece(embedding, weight, bias_vec)

    pull_time = jax.vjp(time_local, time_weight, time_bias)[1]
    grad_time_weight, grad_time_bias = pull_time(jnp.sum(grad_hidden, axis=1))
    pull_one = jax.vjp(
        norm_local, first_conv, sums_one[0], sums_one[1], norm_gain[0], norm_bias[0]
    )[1]
    grad_first, grad_first_sum, grad_second_sum, gain_grad_one, bias_grad_one = pull_one(
        grad_hidden
    )
    grad_first = grad_first + group_return(first_conv, mask_row, grad_first_sum, grad_second_sum)
    pull_conv = jax.vjp(conv_piece, padded_one, conv_first)[1]
    grad_padded, grad_conv_first = pull_conv(grad_first)
    grad_inputs = (rim_return(grad_padded) + grad_masked) * column
    grads = (
        grad_conv_first,
        grad_conv_second,
        grad_res,
        jnp.stack([gain_grad_one, gain_grad_two]),
        jnp.stack([bias_grad_one, bias_grad_two]),
        grad_time_weight,
        grad_time_bias,
    )
    return (grad_inputs, grads)


def block_forward(value_in, key_mask, first_weights, later_weights):
    queries, key_here, value_here = attend_in(
        value_in, first_weights[0], first_weights[1], first_weights[2]
    )
    key_full, value_full = (
        lax.all_gather(key_here, "seq", axis=1, tiled=True),
        lax.all_gather(value_here, "seq", axis=1, tiled=True),
    )
    result = attend_out(value_in, queries, key_full, value_full, key_mask, later_weights)
    kept_pair = (key_full, value_full)
    return (result, (value_in, queries, kept_pair))


def block_backward(grad_out, saved, key_mask, first_weights, later_weights):
    value_in, queries, kept_pair = saved
    key_full, value_full = kept_pair

    def attend_local(current, query_in, key_in, value_full_in, weights_in):
        return attend_out(current, query_in, key_in, value_full_in, key_mask, weights_in)

    pull_out = jax.vjp(attend_local, value_in, queries, key_full, value_full, later_weights)[1]
    grad_value, grad_queries, grad_keys, grad_values, grad_later = pull_out(grad_out)
    grad_keys, grad_values = (
        lax.psum_scatter(grad_keys, "seq", scatter_dimension=1, tiled=True),
        lax.psum_scatter(grad_values, "seq", scatter_dimension=1, tiled=True),
    )
    pull_in = jax.vjp(attend_in, value_in, first_weights[0], first_weights[1], first_weights[2])[1]
    grad_input, grad_gain, grad_bias, grad_qkv = pull_in((grad_queries, grad_keys, grad_values))
    return (grad_value + grad_input, (grad_gain, grad_bias, grad_qkv), grad_later)


def shrink_forward(value_in, mask_row, weight, bias_vec):
    masked = value_in * mask_row[:, :, None]
    carried = shifted(masked[:, -1:], "seq", 1)
    padded = jnp.concatenate([carried, masked], axis=1)
    return (shrink_piece(padded, weight, bias_vec), padded)


def shrink_backward(grad_out, padded, mask_row, weight, bias_vec):
    pull_back = jax.vjp(shrink_piece, padded, weight, bias_vec)[1]
    grad_padded, grad_weight, grad_bias = pull_back(grad_out)
    returned = shifted(grad_padded[:, :1], "seq", -1)
    grad_masked = grad_padded[:, 1:].at[:, -1:].add(returned)
    return (grad_masked * mask_row[:, :, None], grad_weight, grad_bias)


def local(
    frames,
    flow_embed,
    lengths,
    cotangent,
    conv_one,
    conv_two,
    res_weight,
    norm_gain,
    norm_bias,
    time_weight,
    time_bias,
    layer_gain,
    layer_bias,
    qkv_weight,
    out_weight,
    out_bias,
    up_weight,
    up_bias,
    snake_alpha,
    snake_beta,
    down_weight,
    down_bias,
    shrink_weight,
    shrink_bias,
):
    stacked = tuple(
        (
            weight_in.astype(jnp.float32)
            for weight_in in (
                conv_one,
                conv_two,
                res_weight,
                norm_gain,
                norm_bias,
                time_weight,
                time_bias,
                layer_gain,
                layer_bias,
                qkv_weight,
                out_weight,
                out_bias,
                up_weight,
                up_bias,
                snake_alpha,
                snake_beta,
                down_weight,
                down_bias,
            )
        )
    )
    shrink_w = shrink_weight.astype(jnp.float32)
    shrink_b = shrink_bias.astype(jnp.float32)
    seq_count = lax.axis_size("seq")
    seq_index = lax.axis_index("seq")
    frames_one = frames.shape[1]
    frames_two = frames_one // 2
    group_width = frames.shape[2] // GROUPS
    place_one = seq_index * frames_one + jnp.arange(frames_one, dtype=jnp.int32)
    place_two = seq_index * frames_two + jnp.arange(frames_two, dtype=jnp.int32)
    mask_one = (place_one[None, :] < lengths[:, None]).astype(jnp.float32)
    mask_two = (2 * place_two[None, :] < lengths[:, None]).astype(jnp.float32)
    keys_one = (
        jnp.arange(frames_one * seq_count, dtype=jnp.int32)[None, :] < lengths[:, None]
    ).astype(jnp.float32)
    keys_two = (
        2 * jnp.arange(frames_two * seq_count, dtype=jnp.int32)[None, :] < lengths[:, None]
    ).astype(jnp.float32)
    counts_one = (lengths * group_width).astype(jnp.float32)
    counts_two = ((lengths + 1) // 2 * group_width).astype(jnp.float32)
    res_zero, first_zero, later_zero = layer_weights(stacked, 0)
    res_one, first_one, later_one = layer_weights(stacked, 1)
    current, saved_first = resnet_forward(frames, mask_one, counts_one, flow_embed, res_zero)
    current, saved_second = block_forward(current, keys_one, first_zero, later_zero)
    current, saved_shrink = shrink_forward(current, mask_one, shrink_w, shrink_b)
    current, saved_third = resnet_forward(current, mask_two, counts_two, flow_embed, res_one)
    current, saved_fourth = block_forward(current, keys_two, first_one, later_one)
    output = current * mask_two[:, :, None]
    grad_now = cotangent * mask_two[:, :, None]
    grad_now, first_grads, later_grads = block_backward(
        grad_now, saved_fourth, keys_two, first_one, later_one
    )
    grad_now, resnet_grads = resnet_backward(
        grad_now, saved_third, mask_two, counts_two, flow_embed, res_one
    )
    grads_top = layer_grads(resnet_grads, first_grads, later_grads)
    shapes = [array_in.shape for array_in in grads_top]
    top_size = sum((math.prod(shape_in) for shape_in in shapes))
    grad_now, grad_shrink_w, grad_shrink_b = shrink_backward(
        grad_now, saved_shrink, mask_one, shrink_w, shrink_b
    )
    grad_now, first_grads, later_grads = block_backward(
        grad_now, saved_second, keys_one, first_zero, later_zero
    )
    grad_now, resnet_grads = resnet_backward(
        grad_now, saved_first, mask_one, counts_one, flow_embed, res_zero
    )
    grads_low = layer_grads(resnet_grads, first_grads, later_grads)
    low_flat = jnp.concatenate([flatten_all(grads_low), grad_shrink_w.reshape(-1), grad_shrink_b])
    summed_all = lax.psum(jnp.concatenate([flatten_all(grads_top), low_flat]), ("dp", "seq"))
    summed_top = summed_all[:top_size]
    summed_low = summed_all[top_size:]
    parts_top = unflatten_all(summed_top, shapes)
    parts_low = unflatten_all(summed_low, shapes + [shrink_w.shape, shrink_b.shape])
    grads_out = tuple(
        (jnp.stack([parts_low[number], parts_top[number]]) for number in range(len(shapes)))
    )
    return (output, grad_now) + grads_out + (parts_low[-2], parts_low[-1])


def solution(mesh):
    return jax.shard_map(
        local,
        mesh=mesh,
        in_specs=(
            P("dp", "seq", None),
            P("dp", None),
            P("dp"),
            P("dp", "seq", None),
            P(),
            P(),
            P(),
            P(),
            P(),
            P(),
            P(),
            P(),
            P(),
            P(),
            P(),
            P(),
            P(),
            P(),
            P(),
            P(),
            P(),
            P(),
            P(),
            P(),
        ),
        out_specs=(
            P("dp", "seq", None),
            P("dp", "seq", None),
            P(),
            P(),
            P(),
            P(),
            P(),
            P(),
            P(),
            P(),
            P(),
            P(),
            P(),
            P(),
            P(),
            P(),
            P(),
            P(),
            P(),
            P(),
            P(),
            P(),
        ),
        check_vma=False,
    )
```

profile of v0, /device:TPU:0, one launch (start us, length us, event | category | flops | bytes accessed | tf_op | source)
XLA Modules:
  0.0 1183.8 jit_solution(6031716785275706847)
XLA Ops:
  26.0 18.9 %all-reduce.43 = (f32[4,8]{1,0:T(4,128)S(1)}, f32[4,8]{1,0:T(4,128)S(1)}) all-reduce(f32[4,8]{1,0:T(4,128)S(1)} %reduce_sum.812, f32[4,8]{1,0:T(4,128)S(1)} %reduce_sum.806), channel_id=1, replica_groups=mesh['dp'=4,'seq'=8] {'seq'}, use_global_device_ids=true, to_apply=%region_5.6 | all-reduce | flops 64 | bytes 512 | tf_op jit(solution)/shard_map/psum | solution.py:227
  56.2 14.6 %all-reduce.42 = (f32[4,8]{1,0:T(4,128)S(1)}, f32[4,8]{1,0:T(4,128)S(1)}) all-reduce(f32[4,8]{1,0:T(4,128)S(1)} %reduce_sum.821, f32[4,8]{1,0:T(4,128)S(1)} %reduce_sum.818), channel_id=1, replica_groups=mesh['dp'=4,'seq'=8] {'seq'}, use_global_device_ids=true, to_apply=%region_11.12 | all-reduce | flops 64 | bytes 512 | tf_op jit(solution)/shard_map/psum | solution.py:227
  85.6 37.9 %all-gather.7.cloned.1.call-done = f32[4,2048,128]{2,1,0:T(8,128)} async-done(((f32[4,256,128]{2,1,0:T(8,128)}), f32[4,2048,128]{2,1,0:T(8,128)}) %all-gather.7.cloned.1.call-update) | async-done | bytes 4194320 | tf_op jit(solution)/shard_map/all_gather | solution.py:310
  123.5 5.4 copy.128
  128.9 16.6 %fusion.1 = (f32[4,2,256]{2,1,0:T(2,128)S(1)}, f32[4,2,256,2048]{3,2,1,0:T(8,128)S(1)}) fusion(pred[4,2048]{1,0:T(4,128)(4,1)S(1)} %convert_compare_fusion, f32[4,256,2,64]{1,3,2,0:T(8,128)S(1)} %bitcast.540, f32[4,2048,2,64]{1,3,2,0:T(8,128)} %bitcast.513), kind=kOutput, calls=%fused_computation.7 | convolution fusion | flops 3233806336 | bytes 21512192 | tf_op jit(solution)/shard_map/uqhd,ukhd->uhqk/dot_general | solution.py:121
  145.5 5.8 copy-done
  151.3 3.7 fusion.70
  155.1 16.5 %all-gather.5.cloned.1.call-done = f32[4,2048,128]{2,1,0:T(8,128)} async-done(((f32[4,256,128]{2,1,0:T(8,128)}), f32[4,2048,128]{2,1,0:T(8,128)}) %all-gather.5.cloned.1.call-update) | async-done | bytes 4194320 | tf_op jit(solution)/shard_map/all_gather | solution.py:311
  171.6 5.4 copy.126
  177.1 23.0 %fusion.13 = f32[4,2,64,256]{3,2,1,0:T(8,128)S(1)} fusion(f32[4,2048,2,64]{1,3,2,0:T(8,128)} %bitcast.516, f32[4,2,256]{2,1,0:T(2,128)S(1)} %fusion.70, f32[4,2,256,2048]{3,2,1,0:T(8,128)} %copy-done, f32[4,2,256]{2,1,0:T(2,128)S(1)} %get-tuple-element.370, pred[4,2048]{1,0:T(4,128)(4,1)S(1)} %convert_compare_fusion), kind=kOutput, calls=%fused_computation.20 | convolution fusion | flops 3238002688 | bytes 21520384 | tf_op jit(solution)/shard_map/uhqk,ukhd->uqhd/dot_general | solution.py:128
  203.5 16.2 %fusion.30 = f32[4,256,256]{2,1,0:T(8,128)S(1)} fusion(f32[4,256,256]{2,1,0:T(8,128)S(1)} %get-tuple-element.373, f32[256]{0:T(256)S(1)} %bitcast.669, f32[4,256]{1,0:T(4,128)S(1)} %compare_convert_fusion, f32[4,256,1024]{2,1,0:T(8,128)S(1)} %fusion.64, f32[1024]{0:T(1024)S(1)} %copy-done.239, f32[1024]{0:T(1024)S(1)} %bitcast.590, f32[1024]{0:T(1024)S(1)} %bitcast.653, ...), kind=kOutput, calls=%fused_computation.90 | convolution fusion | flops 3227254784 | bytes 6833152 | tf_op jit(solution)/shard_map/ufe,ec->ufc/dot_general | solution.py:139
  241.8 15.1 %all-reduce.41 = (f32[4,8]{1,0:T(4,128)S(1)}, f32[4,8]{1,0:T(4,128)S(1)}) all-reduce(f32[4,8]{1,0:T(4,128)S(1)} %reduce_sum.841, f32[4,8]{1,0:T(4,128)S(1)} %reduce_sum.835), channel_id=1, replica_groups=mesh['dp'=4,'seq'=8] {'seq'}, use_global_device_ids=true, to_apply=%region_23.24 | all-reduce | flops 64 | bytes 512 | tf_op jit(solution)/shard_map/psum | solution.py:227
  273.0 14.3 %all-reduce.40 = (f32[4,8]{1,0:T(4,128)}, f32[4,8]{1,0:T(4,128)}) all-reduce(f32[4,8]{1,0:T(4,128)} %reduce_sum.853, f32[4,8]{1,0:T(4,128)} %reduce_sum.847), channel_id=1, replica_groups=mesh['dp'=4,'seq'=8] {'seq'}, use_global_device_ids=true, to_apply=%region_29.30 | all-reduce | flops 64 | bytes 512 | tf_op jit(solution)/shard_map/psum | solution.py:227
  302.9 22.7 %all-gather.11.cloned.1.call-done = f32[4,1024,128]{2,1,0:T(8,128)} async-done(((f32[4,128,128]{2,1,0:T(8,128)}), f32[4,1024,128]{2,1,0:T(8,128)}) %all-gather.11.cloned.1.call-update) | async-done | bytes 2097168 | tf_op jit(solution)/shard_map/all_gather | solution.py:310
  328.5 5.5 fusion.15
  337.1 19.2 %all-gather.9.cloned.1.call-done = f32[4,1024,128]{2,1,0:T(8,128)} async-done(((f32[4,128,128]{2,1,0:T(8,128)}), f32[4,1024,128]{2,1,0:T(8,128)}) %all-gather.9.cloned.1.call-update) | async-done | bytes 2097168 | tf_op jit(solution)/shard_map/all_gather | solution.py:311
  356.3 3.3 copy.130
  359.6 8.2 fusion.27
  369.8 9.9 multiply_reduce_fusion.4
  385.9 4.6 fusion.26
  393.7 8.4 convert_reduce_fusion.1
  405.9 4.6 fusion.17
  414.4 12.1 %convolution_bitcast_fusion = f32[128,2,8,128]{3,2,1,0:T(8,128)S(1)} fusion(f32[4,128,256]{2,1,0:T(8,128)} %param.47, f32[4,128]{1,0:T(4,128)S(1)} %compare_convert_fusion.1, f32[4,128,1024]{2,1,0:T(8,128)} %copy-done.84, f32[1024]{0:T(1024)S(1)} %get-tuple-element.335, f32[1024]{0:T(1024)S(1)} %bitcast.587, f32[1024]{0:T(1024)S(1)} %bitcast.651), kind=kOutput, calls=%fused_computation.80 | convolution fusion | flops 1613365248 | bytes 3684352 | tf_op jit(solution)/shard_map/transpose(jvp(ufe,ec->ufc))/dot_general | solution.py:139
  432.8 6.2 fusion.16
  440.8 24.8 %reduce-scatter.7.cloned.1.call-done = f32[4,128,128]{2,1,0:T(8,128)} async-done(((f32[4,1024,128]{2,1,0:T(8,128)}), f32[4,128,128]{2,1,0:T(8,128)}) %reduce-scatter.7.cloned.1.call-update) | async-done | bytes 262160 | tf_op jit(solution)/shard_map/reduce_scatter | solution.py:328
  469.7 3.6 multiply_reduce_fusion.27
  474.4 14.8 %all-reduce.39 = (f32[4,8]{1,0:T(4,128)S(1)}, f32[4,8]{1,0:T(4,128)S(1)}) all-reduce(f32[4,8]{1,0:T(4,128)S(1)} %get-tuple-element.331, f32[4,8]{1,0:T(4,128)S(1)} %get-tuple-element.330), channel_id=1, replica_groups=mesh['dp'=4,'seq'=8] {'seq'}, use_global_device_ids=true, to_apply=%region_50.52 | all-reduce | flops 64 | bytes 512 | tf_op jit(solution)/shard_map/psum | solution.py:231
  520.6 15.2 %all-reduce.38 = (f32[4,8]{1,0:T(4,128)S(1)}, f32[4,8]{1,0:T(4,128)S(1)}) all-reduce(f32[4,8]{1,0:T(4,128)S(1)} %get-tuple-element.329, f32[4,8]{1,0:T(4,128)S(1)} %get-tuple-element.328), channel_id=1, replica_groups=mesh['dp'=4,'seq'=8] {'seq'}, use_global_device_ids=true, to_apply=%region_56.58 | all-reduce | flops 64 | bytes 512 | tf_op jit(solution)/shard_map/psum | solution.py:231
  557.4 4.3 pad.136
  561.7 4.3 pad.137
  571.2 21.0 %multiply_reduce_fusion.1 = (f32[1024]{0:T(1024)}, f32[1024]{0:T(1024)}, f32[1024]{0:T(1024)}, f32[4,256,1024]{2,1,0:T(8,128)S(1)}) fusion(f32[4,256,1024]{2,1,0:T(8,128)} %copy-done.53, f32[1024]{0:T(1024)S(1)} %copy-done.242, f32[1024]{0:T(1024)S(1)} %bitcast.591, f32[1024]{0:T(1024)S(1)} %bitcast.654, f32[1024]{0:T(1024)S(1)} %copy-done.240, ...), kind=kOutput, calls=%fused_computation.21 | convolution fusion | flops 3237213184 | bytes 9994240 | tf_op jit(solution)/shard_map/transpose(jvp(ufe,ec->ufc))/dot_general | solution.py:139
  598.3 14.9 %fusion.12 = f32[4,2,64,2048]{3,2,1,0:T(8,128)} fusion(f32[4,2,64,256]{3,2,1,0:T(8,128)S(1)} %convolution_bitcast_fusion.6, f32[4,2,256]{2,1,0:T(2,128)S(1)} %copy-done.124, f32[4,2,256,2048]{3,2,1,0:T(8,128)S(1)} %bitcast.510, f32[4,2,256]{2,1,0:T(2,128)S(1)} %copy-done.119, pred[4,2048]{1,0:T(4,128)(4,1)S(1)} %convert_compare_fusion), kind=kOutput, calls=%fused_computation.19 | convolution fusion | flops 3238002688 | bytes 21520384 | tf_op jit(solution)/shard_map/transpose(jvp(uhqk,ukhd->uqhd))/dot_general | solution.py:128
  613.2 5.7 copy.137
  625.9 26.9 %convert_reduce_fusion = (f32[4,2,256]{2,1,0:T(2,128)S(1)}, pred[4,2,256,2048]{3,2,1,0:T(32,128)(4,1)}, f32[4,2,256]{2,1,0:T(2,128)S(1)}, f32[4,2,256,2048]{3,2,1,0:T(8,128)}) fusion(f32[4,2,256]{2,1,0:T(2,128)S(1)} %copy-done.119, f32[4,2,256,2048]{3,2,1,0:T(8,128)} %copy-done, pred[4,2048]{1,0:T(4,128)(4,1)S(1)} %convert_compare_fusion, ...), kind=kOutput, calls=%fused_computation.1 | convolution fusion | flops 3258970112 | bytes 42508288 | tf_op jit(solution)/shard_map/transpose(jvp(uhqk,ukhd->uqhd))/dot_general | solution.py:128
  652.9 12.7 %fusion.334 = (f32[4,2,256]{2,1,0:T(2,128)S(1)}, f32[4,2,256,2048]{3,2,1,0:T(8,128)S(1)}) fusion(f32[4,2,256]{2,1,0:T(2,128)S(1)} %copy-done.119, f32[4,2,256,2048]{3,2,1,0:T(8,128)} %copy-done, pred[4,2048]{1,0:T(4,128)(4,1)S(1)} %convert_compare_fusion, f32[4,2,256]{2,1,0:T(2,128)S(1)} %neg.107, f32[4,2,256,2048]{3,2,1,0:T(8,128)} %get-tuple-element.386, ...), kind=kLoop, calls=%fused_computation.646 | loop fusion | flops 29358080 | bytes 50372608 | tf_op jit(solution)/shard_map/transpose(jvp())/reduce_sum | solution.py:125
  665.6 18.7 %fusion.3 = f32[4,2,2048,64]{2,3,1,0:T(8,128)} fusion(f32[4,256,2,64]{1,3,2,0:T(8,128)S(1)} %bitcast.541, f32[4,2,256,2048]{3,2,1,0:T(8,128)S(1)} %get-tuple-element.224, pred[4,2,256,2048]{3,2,1,0:T(32,128)(4,1)} %get-tuple-element.226, f32[4,2,256]{2,1,0:T(2,128)S(1)} %bitcast.617, pred[4,2048]{1,0:T(4,128)(4,1)S(1)} %convert_compare_fusion), kind=kOutput, calls=%fused_computation.9 | convolution fusion | flops 3238002688 | bytes 25706496 | tf_op jit(solution)/shard_map/transpose(jvp(uqhd,ukhd->uhqk))/dot_general | solution.py:121
  684.3 5.3 copy.138
  716.1 21.2 %convolution_bitcast_fusion.2 = f32[128,2,8,128]{3,2,1,0:T(8,128)S(1)} fusion(f32[4,256,256]{2,1,0:T(8,128)S(1)} %copy-done.30, f32[4,256]{1,0:T(4,128)S(1)} %compare_convert_fusion, f32[4,256,1024]{2,1,0:T(8,128)S(1)} %copy-done.54, f32[1024]{0:T(1024)S(1)} %copy-done.241, f32[1024]{0:T(1024)S(1)} %bitcast.592, f32[1024]{0:T(1024)S(1)} %bitcast.655), kind=kOutput, calls=%fused_computation.82 | convolution fusion | flops 3226730496 | bytes 6307840 | tf_op jit(solution)/shard_map/transpose(jvp(ufe,ec->ufc))/dot_general | solution.py:139
  738.8 4.0 convolution_bitcast_fusion.3
  745.4 23.1 %fusion.2 = f32[4,2,256,64]{2,3,1,0:T(8,128)S(1)} fusion(f32[4,2048,2,64]{1,3,2,0:T(8,128)S(1)} %bitcast.514, f32[4,2,256,2048]{3,2,1,0:T(8,128)} %copy-done.15, pred[4,2,256,2048]{3,2,1,0:T(32,128)(4,1)S(1)} %copy-done.270, f32[4,2,256]{2,1,0:T(2,128)S(1)} %bitcast.618, pred[4,2048]{1,0:T(4,128)(4,1)S(1)} %convert_compare_fusion), kind=kOutput, calls=%fused_computation.8 | convolution fusion | flops 3238002688 | bytes 25706496 | tf_op jit(solution)/shard_map/transpose(jvp(uqhd,ukhd->uhqk))/dot_general | solution.py:121
  772.8 4.6 multiply_reduce_fusion.10
  777.9 15.8 %all-reduce.37 = (f32[4,8]{1,0:T(4,128)S(1)}, f32[4,8]{1,0:T(4,128)S(1)}) all-reduce(f32[4,8]{1,0:T(4,128)S(1)} %get-tuple-element.327, f32[4,8]{1,0:T(4,128)S(1)} %get-tuple-element.326), channel_id=1, replica_groups=mesh['dp'=4,'seq'=8] {'seq'}, use_global_device_ids=true, to_apply=%region_71.74 | all-reduce | flops 64 | bytes 512 | tf_op jit(solution)/shard_map/psum | solution.py:231
  830.7 4.3 multiply_reduce_fusion.20
  838.7 15.0 %all-reduce.36 = (f32[4,8]{1,0:T(4,128)S(1)}, f32[4,8]{1,0:T(4,128)S(1)}) all-reduce(f32[4,8]{1,0:T(4,128)S(1)} %get-tuple-element.325, f32[4,8]{1,0:T(4,128)S(1)} %get-tuple-element.324), channel_id=1, replica_groups=mesh['dp'=4,'seq'=8] {'seq'}, use_global_device_ids=true, to_apply=%region_77.80 | all-reduce | flops 64 | bytes 512 | tf_op jit(solution)/shard_map/psum | solution.py:231
  897.7 10.4 fusion.35
  916.8 201.8 %all-reduce.46.cloned.1.call-done = f32[2961152]{0:T(1024)} async-done(((f32[2961152]{0:T(1024)}), f32[2961152]{0:T(1024)}) %all-reduce.46.cloned.1.call-update) | async-done | bytes 11844624 | tf_op jit(solution)/shard_map/psum | solution.py:450
  1128.9 4.5 fusion.350
  1136.0 4.1 fusion.349
  (988 shorter events, 386.5 us)
Async XLA Ops:
  7.2 116.3 %all-gather.7.cloned.1.call-start = ((), (), s32[]{:S(2)}) async-start(), calls=%async_computation.5 | async-start | bytes 4718592 | tf_op jit(solution)/shard_map/all_gather | solution.py:310
  9.5 62.8 %copy-start.1 = (f32[4,256,256]{2,1,0:T(8,128)}, f32[4,256,256]{2,1,0:T(8,128)S(1)}, u32[]{:S(2)}) copy-start(f32[4,256,256]{2,1,0:T(8,128)S(1)} %broadcast_multiply_fusion) | copy-start | bytes 3145732
  9.5 14.4 %collective-permute-start = (f32[4,1,256]{2,1,0:T(1,128)S(1)}, f32[4,1,256]{2,1,0:T(1,128)S(1)}, u32[]{:S(2)}, u32[]{:S(2)}) collective-permute-start(f32[4,1,256]{2,1,0:T(1,128)S(1)} %get-tuple-element.304), channel_id=1, source_target_pairs={{0,1},{1,2},{2,3},{3,4},{4,5},{5,6},{6,7},{8,9},{9,10},{10,11},{11... | collective-permute-start | bytes 12296 | tf_op jit(solution)/shard_map/ppermute | solution.py:23
  11.9 10.5 collective-permute-start.1
  15.9 30.0 %copy-start.161 = (f32[1,1,256]{2,1,0:T(1,128)}, f32[1,1,256]{2,1,0:T(1,128)S(1)}, u32[]{:S(2)}) copy-start(f32[1,1,256]{2,1,0:T(1,128)S(1)} %get-tuple-element.353) | copy-start | bytes 3076
  17.2 28.7 %copy-start.191 = (f32[1,1,256]{2,1,0:T(1,128)}, f32[1,1,256]{2,1,0:T(1,128)S(1)}, u32[]{:S(2)}) copy-start(f32[1,1,256]{2,1,0:T(1,128)S(1)} %get-tuple-element.357) | copy-start | bytes 3076
  18.5 56.6 %copy-start.158 = (f32[1,1,256]{2,1,0:T(1,128)}, f32[1,1,256]{2,1,0:T(1,128)S(1)}, u32[]{:S(2)}) copy-start(f32[1,1,256]{2,1,0:T(1,128)S(1)} %get-tuple-element.345) | copy-start | bytes 3076
  25.7 29.4 %copy-start.25 = (f32[4,256,256]{2,1,0:T(8,128)}, f32[4,256,256]{2,1,0:T(8,128)S(1)}, u32[]{:S(2)}) copy-start(f32[4,256,256]{2,1,0:T(8,128)S(1)} %get-tuple-element.366) | copy-start | bytes 3145732
  46.8 6.0 collective-permute-start.2
  48.1 3.1 collective-permute-start.3
  74.6 125.5 %copy-start.10 = (f32[4,256,256]{2,1,0:T(8,128)}, f32[4,256,256]{2,1,0:T(8,128)S(1)}, u32[]{:S(2)}) copy-start(f32[4,256,256]{2,1,0:T(8,128)S(1)} %get-tuple-element.369) | copy-start | bytes 3145732
  78.0 93.6 %all-gather.5.cloned.1.call-start = ((), (), s32[]{:S(2)}) async-start(), calls=%async_computation.4 | async-start | bytes 4718592 | tf_op jit(solution)/shard_map/all_gather | solution.py:311
  78.8 246.9 %all-gather.11.cloned.1.call-start = ((), (), s32[]{:S(2)}) async-start(), calls=%async_computation.7 | async-start | bytes 2359296 | tf_op jit(solution)/shard_map/all_gather | solution.py:310
  79.7 471.0 %copy-start.107 = (f32[4,128]{1,0:T(4,128)}, f32[4,128]{1,0:T(4,128)S(1)}, u32[]{:S(2)}) copy-start(f32[4,128]{1,0:T(4,128)S(1)} %compare_convert_fusion.1) | copy-start | bytes 6148
  85.6 43.4 %copy-start.80 = (f32[4,256,128]{1,2,0:T(8,128)}, f32[4,256,128]{1,2,0:T(8,128)S(1)}, u32[]{:S(2)}) copy-start(f32[4,256,128]{1,2,0:T(8,128)S(1)} %copy.127) | copy-start | bytes 1572868
  145.5 31.5 %copy-start.118 = (f32[4,2,256]{2,1,0:T(2,128)}, f32[4,2,256]{2,1,0:T(2,128)S(1)}, u32[]{:S(2)}) copy-start(f32[4,2,256]{2,1,0:T(2,128)S(1)} %get-tuple-element.370) | copy-start | bytes 24580
  220.9 6.3 collective-permute-start.4
  228.3 28.6 %copy-start.220 = (f32[4]{0:T(128)S(1)}, f32[4]{0:T(128)}, u32[]{:S(2)}) copy-start(f32[4]{0:T(128)} %get-tuple-element.364) | copy-start | bytes 52
  228.3 29.5 %copy-start.189 = (f32[1,1,256]{2,1,0:T(1,128)S(1)}, f32[1,1,256]{2,1,0:T(1,128)}, u32[]{:S(2)}) copy-start(f32[1,1,256]{2,1,0:T(1,128)} %get-tuple-element.351) | copy-start | bytes 3076
  228.3 29.5 %copy-start.192 = (f32[1,1,256]{2,1,0:T(1,128)S(1)}, f32[1,1,256]{2,1,0:T(1,128)}, u32[]{:S(2)}) copy-start(f32[1,1,256]{2,1,0:T(1,128)} %get-tuple-element.355) | copy-start | bytes 3076
  228.3 29.5 %copy-start.225 = (f32[4,256]{1,0:T(4,128)S(1)}, f32[4,256]{1,0:T(4,128)}, u32[]{:S(2)}) copy-start(f32[4,256]{1,0:T(4,128)} %convolution_add_fusion.13) | copy-start | bytes 12292
  232.3 5.6 collective-permute-start.6
  234.9 4.4 collective-permute-start.5
  241.4 52.1 %copy-start.40 = (f32[4,128,256]{2,1,0:T(8,128)}, f32[4,128,256]{2,1,0:T(8,128)S(1)}, u32[]{:S(2)}) copy-start(f32[4,128,256]{2,1,0:T(8,128)S(1)} %get-tuple-element.374) | copy-start | bytes 1572868
  258.3 5.8 collective-permute-start.8
  260.9 4.6 collective-permute-start.7
  267.5 61.0 %copy-start.44 = (f32[4,128,256]{2,1,0:T(8,128)}, f32[4,128,256]{2,1,0:T(8,128)S(1)}, u32[]{:S(2)}) copy-start(f32[4,128,256]{2,1,0:T(8,128)S(1)} %get-tuple-element.375) | copy-start | bytes 1572868
  298.2 58.1 %all-gather.9.cloned.1.call-start = ((), (), s32[]{:S(2)}) async-start(), calls=%async_computation.6 | async-start | bytes 2359296 | tf_op jit(solution)/shard_map/all_gather | solution.py:311
  298.8 142.0 %reduce-scatter.5.cloned.1.call-start = ((), (), s32[]{:S(2)}) async-start(), calls=%async_computation.8 | async-start | bytes 2359296 | tf_op jit(solution)/shard_map/reduce_scatter | solution.py:329
  299.6 104.3 %copy-start.111 = (pred[4,1024]{1,0:T(4,128)(4,1)}, pred[4,1024]{1,0:T(4,128)(4,1)S(1)}, u32[]{:S(2)}) copy-start(pred[4,1024]{1,0:T(4,128)(4,1)S(1)} %convert_compare_fusion.1) | copy-start | bytes 12292
  300.3 114.1 %copy-start.237 = (f32[1024]{0:T(1024)}, f32[1024]{0:T(1024)S(1)}, u32[]{:S(2)}) copy-start(f32[1024]{0:T(1024)S(1)} %get-tuple-element.335) | copy-start | bytes 12292
  368.4 59.7 %copy-start.12 = (f32[4,128,256]{2,1,0:T(8,128)}, f32[4,128,256]{2,1,0:T(8,128)S(1)}, u32[]{:S(2)}) copy-start(f32[4,128,256]{2,1,0:T(8,128)S(1)} %get-tuple-element.381) | copy-start | bytes 1572868
  393.4 72.2 %reduce-scatter.7.cloned.1.call-start = ((), (), s32[]{:S(2)}) async-start(), calls=%async_computation.9 | async-start | bytes 2359296 | tf_op jit(solution)/shard_map/reduce_scatter | solution.py:328
  413.3 355.5 %reduce-scatter.9.cloned.1.call-start = ((), (), s32[]{:S(2)}) async-start(), calls=%async_computation.10 | async-start | bytes 4718592 | tf_op jit(solution)/shard_map/reduce_scatter | solution.py:329
  432.0 33.5 %copy-start.87 = (bf16[2,256,384]{2,1,0:T(8,128)(2,1)S(1)}, bf16[2,256,384]{2,1,0:T(8,128)(2,1)}, u32[]{:S(2)}) copy-start(bf16[2,256,384]{2,1,0:T(8,128)(2,1)} %param.57) | copy-start | bytes 1179652
  432.8 37.0 %copy-start.43 = (f32[4,128,256]{2,1,0:T(8,128)S(1)}, f32[4,128,256]{2,1,0:T(8,128)}, u32[]{:S(2)}) copy-start(f32[4,128,256]{2,1,0:T(8,128)} %copy-done.41) | copy-start | bytes 1572868
  498.1 15.8 %collective-permute-start.9 = (f32[4,1,256]{2,1,0:T(1,128)S(1)}, f32[4,1,256]{2,1,0:T(1,128)S(1)}, u32[]{:S(2)}, u32[]{:S(2)}) collective-permute-start(f32[4,1,256]{2,1,0:T(1,128)S(1)} %get-tuple-element.293), channel_id=1, source_target_pairs={{0,1},{1,2},{2,3},{3,4},{4,5},{5,6},{6,7},{8,9},{9,10},{10,11},{11... | collective-permute-start | bytes 12296 | tf_op jit(solution)/shard_map/ppermute | solution.py:23
  510.7 4.6 collective-permute-start.10
  544.9 5.7 collective-permute-start.12
  546.3 4.1 collective-permute-start.11
  567.8 3.1 collective-permute-start.13
  597.5 146.4 %copy-start.26 = (f32[4,256,256]{2,1,0:T(8,128)}, f32[4,256,256]{2,1,0:T(8,128)S(1)}, u32[]{:S(2)}) copy-start(f32[4,256,256]{2,1,0:T(8,128)S(1)} %get-tuple-element.215) | copy-start | bytes 3145732
  619.0 149.8 %reduce-scatter.11.cloned.1.call-start = ((), (), s32[]{:S(2)}) async-start(), calls=%async_computation.11 | async-start | bytes 4718592 | tf_op jit(solution)/shard_map/reduce_scatter | solution.py:328
  689.7 428.9 %all-reduce.46.cloned.1.call-start = ((), (), s32[]{:S(2)}) async-start(), calls=%async_computation.12 | async-start | bytes 23691264 | tf_op jit(solution)/shard_map/psum | solution.py:450
  804.5 21.3 %collective-permute-start.14 = (f32[4,1,256]{2,1,0:T(1,128)}, f32[4,1,256]{2,1,0:T(1,128)}, u32[]{:S(2)}, u32[]{:S(2)}) collective-permute-start(f32[4,1,256]{2,1,0:T(1,128)} %get-tuple-element.289), channel_id=1, source_target_pairs={{0,1},{1,2},{2,3},{3,4},{4,5},{5,6},{6,7},{8,9},{9,10},{10,11},{11... | collective-permute-start | bytes 12296 | tf_op jit(solution)/shard_map/ppermute | solution.py:23
  822.3 6.3 collective-permute-start.15
  910.1 3.1 collective-permute-start.16
  911.8 3.1 collective-permute-start.17
  (254 other events, 2534.1 us)
Sparse Core Ops, SparseCore 0:
  78.1 45.3 all-gather.6
  125.7 45.8 all-gather.4
  298.3 27.2 all-gather.10
  327.7 28.5 all-gather.8
  393.5 35.2 reduce-scatter.4
  431.0 34.5 reduce-scatter.6
  619.2 49.9 reduce-scatter.8
  689.8 49.9 reduce-scatter.10
  896.5 222.0 all-reduce.45
where the time goes:
time: 1200 us; the launch traced here: 1180 us
  matrix products  358 us (30%)
  waiting for transfers between devices  327 us (27%)
  local copies, waits for them, and re-layouts  225 us (19%)
  blocking collectives  124 us (10%)
  other arithmetic  99 us (8%)
  starting transfers between devices  33.1 us (3%)
  between operations  18.1 us (2%)
    psum x1, waiting for transfers between devices, local(): lax.psum(jnp.concatenate([flatten_all(grads_top), low_flat]), ('dp', 'seq'))  202 us
    dot_general x6, matrix products, attend_out(): jnp.einsum('ufe,ec->ufc', snake_out, down_weight, precision=precise)  90.9 us
    unnamed x606, local copies, waits for them, and re-layouts  90.1 us
    dot_general x6, matrix products, attend_out(): jnp.einsum('uhqk,ukhd->uqhd', weights_soft, value_heads, precision=precise)  86.1 us
    dot_general x6, matrix products, attend_out(): jnp.einsum('uqhd,ukhd->uhqk', query_heads, key_heads, precision=precise)  74.7 us
    psum x4, blocking collectives, group_total(): return lax.psum((first_sum, second_sum), 'seq')  62.9 us
    psum x4, blocking collectives, group_return(): grad_first, grad_second = lax.psum((grad_first, grad_second), 'seq')  60.8 us
    all_gather x2, waiting for transfers between devices, block_forward(): lax.all_gather(key_here, 'seq', axis=1, tiled=True)  60.6 us
  transfers between devices with their start and end apart: 27, of which 9 were waited for; matrix products, arithmetic and copies ran while one was open for 26% of the time, Pallas kernels for 0%

commit v1 on v0

--- a/solution.py
+++ b/solution.py
@@ -1,8 +1,13 @@
 import math
+import typing
+from types import SimpleNamespace
+from typing import Any
 
 import jax
 import jax.numpy as jnp
 from jax import lax
+from jax.experimental import pallas as pl
+from jax.experimental.pallas import tpu as pltpu
 from jax.sharding import PartitionSpec as P
 
 HEADS = 2
@@ -348,7 +353,7 @@
     return (grad_masked * mask_row[:, :, None], grad_weight, grad_bias)
 
 
-def local(
+def general_local(
     frames,
     flow_embed,
     lengths,
@@ -458,59 +463,1654 @@
     return (output, grad_now) + grads_out + (parts_low[-2], parts_low[-1])
 
 
+F32, BF = jnp.float32, jnp.bfloat16
+MESH = pl.DeviceIdType.MESH
+NN = (((1,), (0,)), ((), ()))
+NT = (((1,), (1,)), ((), ()))
+LOG2E = math.log2(math.e)
+LN2 = math.log(2.0)
+ANY = pl.BlockSpec(memory_space=pl.ANY)
+WHOLE = pl.BlockSpec(memory_space=pltpu.VMEM)
+
+SIN_SQUARE = (
+    9.869604400158673,
+    -32.46969664558586,
+    42.72838511691944,
+    -30.121754360183303,
+    13.206610351651772,
+    -3.913077711416514,
+    0.7419801200174108,
+)
+SIN_TWICE = (
+    6.283185302511503,
+    -41.34170040531735,
+    81.605131385789,
+    -76.703015353733,
+    42.025926985052664,
+    -14.89984666534637,
+    3.238137506736557,
+)
+
+UP, DOWN, OUT, LATER_SMALL = 0, 1024, 2048, 2176
+BUCKET_ROWS = (2304, 3072, 2304, 1280, 1024)
+BUCKET_AT = (0, 2304, 5376, 7680, 8960)
+CORE_AT, CORE_ROWS = (0, 1152, 0, 2688, 3328), 3840
+LATER_AT = (5376, 0)
+CONV_TWO_AT = (7680, 2304)
+RES_AT = (8448, 3072)
+QUERY_KEY_AT = (8704, 3328)
+CONV_ONE_AT = (8960, 3584)
+VALUE_AT = (9728, 4352)
+SMALL_AT = (9856, 4480)
+SHRINK_AT, EMBED_AT = 4504, 5272
+
+
+def pick(total, most):
+    best = 16
+    for size in range(16, most + 1, 16):
+        if total % size == 0:
+            best = size
+    return best
+
+
+def fits(shape, utterances, frames_in):
+    return shape["seq"] == 2 * utterances and frames_in == 256 and shape["dp"] * utterances == 16
+
+
+def split(value):
+    high = value.astype(BF)
+    return high, (value - high.astype(F32)).astype(BF)
+
+
+def dot(left, right, dims=NN):
+    return lax.dot_general(left, right, dims, preferred_element_type=F32)
+
+
+def dot_weight(value, weight, dims=NN):
+    rows = value.shape[0]
+    both = dot(jnp.concatenate(split(value), 0), weight, dims)
+    return both[:rows] + both[rows:]
+
+
+def dot_pair(left, right):
+    rows = left[0].shape[0]
+    both = dot(jnp.concatenate(left, 0), right[0])
+    return both[:rows] + both[rows:] + dot(left[0], right[1])
+
+
+def fold8(value):
+    return jnp.sum(value.reshape(value.shape[0] // 8, 8, value.shape[1]), axis=0)
+
+
+def polynomial(coefficients, at):
+    total = jnp.full_like(at, coefficients[-1])
+    for number in coefficients[-2::-1]:
+        total = total * at + number
+    return total
+
+
+def mish_terms(value):
+    raised = jnp.exp(jnp.minimum(value, 20.0))
+    top = raised * (raised + 2.0)
+    return raised, top, 1.0 / (top + 2.0)
+
+
+def mish_of(value):
+    raised, top, inverse = mish_terms(value)
+    return value * (top * inverse)
+
+
+def mish_slope(value):
+    raised, top, inverse = mish_terms(value)
+    return inverse * (top + 4.0 * value * (raised * (raised + 1.0)) * inverse)
+
+
+def loop(count, body):
+    def step(index, carry):
+        body(index)
+        return carry
+
+    lax.fori_loop(0, count, step, 0)
+
+
+def at8(start, size):
+    return pl.ds(pl.multiple_of(start, 8), size)
+
+
+def at16(start, size):
+    return pl.ds(pl.multiple_of(start, 16), size)
+
+
+class Arguments(typing.NamedTuple):
+    frames: Any
+    flow_embed: Any
+    lengths: Any
+    cotangent: Any
+    conv_one: Any
+    conv_two: Any
+    res_weight: Any
+    norm_gain: Any
+    norm_bias: Any
+    time_weight: Any
+    time_bias: Any
+    layer_gain: Any
+    layer_bias: Any
+    qkv_weight: Any
+    out_weight: Any
+    out_bias: Any
+    up_weight: Any
+    up_bias: Any
+    snake_alpha: Any
+    snake_beta: Any
+    down_weight: Any
+    down_bias: Any
+    shrink_weight: Any
+    shrink_bias: Any
+
+
+def matrices(found):
+    return (
+        found.conv_one,
+        found.conv_two,
+        found.res_weight,
+        found.qkv_weight,
+        found.out_weight,
+        found.up_weight,
+        found.down_weight,
+        found.shrink_weight,
+    )
+
+
+def scratch_of(shape):
+    depth = shape["seq"] // 2
+    own_rows = (256 * depth, 128 * depth)
+
+    def array(*size):
+        return pltpu.VMEM(size, F32)
+
+    def short(*size):
+        return pltpu.VMEM(size, BF)
+
+    def semaphores(*size):
+        return pltpu.SemaphoreType.DMA(size)
+
+    shared = dict(
+        w_conv_one=short(2, 3, 256, 256),
+        w_conv_two=short(2, 3, 256, 256),
+        w_res_weight=short(2, 256, 256),
+        w_qkv_weight=short(2, 256, 384),
+        w_out_weight=short(2, 128, 256),
+        w_up_weight=short(2, 256, 1024),
+        w_down_weight=short(2, 1024, 256),
+        w_shrink_weight=short(3, 256, 256),
+        first=array(2, own_rows[0] + 64, 128),
+        cot=array(own_rows[1], 256),
+        last=array(own_rows[1], 256),
+        dfirst=array(2, own_rows[0], 128),
+        dy=array(own_rows[0], 256),
+        dkr=array(own_rows[0], 256),
+        dx=array(own_rows[0] + 32, 256),
+        da=array(own_rows[1] + 32, 256),
+        vt=short(2, own_rows[0], 256),
+        dd=short(2, own_rows[0], 128),
+        qq=short(2, own_rows[0], 128),
+        tall=array(256, 4 * 256),
+        wide=array(2 * depth, 256, 256),
+        half=short(4 * depth, 256, 256),
+        te=array(2, 8, 256),
+        sums=array(8, 16, 256),
+        sums_in=array(8, 16, 256),
+        stat=array(4, 8, 256),
+        narrow_acc=array(8, 8, 256),
+        wide_acc=array(3, 8, 1024),
+        gather=short(256, 256),
+        grads=array(sum(BUCKET_ROWS), 256),
+        core=array(CORE_ROWS, 256),
+        s_weight=semaphores(16),
+        s_frames=semaphores(4, depth),
+        s_cot=semaphores(2, depth),
+        s_last=semaphores(2, depth),
+        s_grad=semaphores(2, depth),
+        s_sums=semaphores(2, 8),
+        s_kv=semaphores(4, depth),
+        s_first=semaphores(2),
+        s_dk=semaphores(4),
+        s_dx=semaphores(4),
+        s_total=semaphores(len(BUCKET_ROWS), 17),
+    )
+    layers = [
+        dict(
+            a=array(own + 32, 256),
+            c1=array(own + 32, 256),
+            h=array(own + 32, 256),
+            c2=array(own + 32, 256),
+            x=array(own, 256),
+            att=array(own, 128),
+            qh=short(2, own, 256),
+            kv=array(2 * own, 256),
+            kh=short(2, 2 * own, 256),
+            vh=short(2, 2 * own, 256),
+            kt=short(2, own // 128, 128, 256),
+        )
+        for own in own_rows
+    ]
+    arrivals = [
+        dict(
+            near=array(size // 4, 256),
+            next=array(size // 8, 256),
+            far=array(depth - 1, size // 32, 256),
+        )
+        for size in BUCKET_ROWS
+    ]
+    return [shared] + layers + arrivals
+
+
+def named(groups, refs):
+    found, at = [], 0
+    for group in groups:
+        found.append(SimpleNamespace(**dict(zip(group, refs[at : at + len(group)]))))
+        at += len(group)
+    return found
+
+
+def fused_kernel(shape, groups, *refs):
+    inputs = Arguments(*refs[:24])
+    output, input_grad, grad_total = refs[24:27]
+    r, *rest = named(groups, refs[27:])
+    layers, arrivals = rest[:2], rest[2:]
+    dp_count, seq_count = shape["dp"], shape["seq"]
+    depth = seq_count // 2
+    dp, seq = lax.axis_index("dp"), lax.axis_index("seq")
+    member, place = lax.rem(seq, 2), lax.div(seq, 2)
+    partner = seq + 1 - 2 * member
+    half = depth
+    own_rows = (256 * depth, 128 * depth)
+    utterance = dp * depth + place
+    length = inputs.lengths[place]
+    lane128 = lax.broadcasted_iota(jnp.int32, (1, 128), 1)
+    low_half = lane128 < 64
+
+    def there(index):
+        return {"dp": dp, "seq": index}
+
+    def remote(source, target, sent, arrived, device):
+        return pltpu.make_async_remote_copy(
+            source, target, sent, arrived, device_id=device, device_id_type=MESH
+        )
+
+    held = (
+        r.w_conv_one,
+        r.w_conv_two,
+        r.w_res_weight,
+        r.w_qkv_weight,
+        r.w_out_weight,
+        r.w_up_weight,
+        r.w_down_weight,
+        r.w_shrink_weight,
+    )
+    weight_copies = [
+        pltpu.make_async_copy(matrix, target, r.s_weight.at[number])
+        for number, (matrix, target) in enumerate(zip(matrices(inputs), held))
+    ]
+    time_copies = []
+    for layer in (0, 1):
+        for part in range(4):
+            time_copies.append(
+                pltpu.make_async_copy(
+                    inputs.time_weight.at[layer, pl.ds(256 * part, 256)],
+                    r.half.at[4 * layer + part],
+                    r.s_weight.at[len(held) + 4 * layer + part],
+                )
+            )
+    for copy in time_copies + weight_copies:
+        copy.start()
+
+    def zero(ref, start, size):
+        ref[pl.ds(start, size), :] = jnp.zeros((size, ref.shape[1]), F32)
+
+    for mine, own in zip(layers, own_rows):
+        for ref in (mine.a, mine.h, mine.c2):
+            zero(ref, 0, 16)
+            zero(ref, own + 16, 16)
+    for part in (0, 1):
+        zero(r.first.at[part], 0, 32)
+        zero(r.first.at[part], own_rows[0] + 32, 32)
+    zero(r.da, 0, 16)
+    zero(r.da, own_rows[1] + 16, 16)
+    for start in (0, own_rows[1] + 16, own_rows[0] + 16):
+        zero(r.dx, start, 16)
+
+    barrier = pltpu.get_barrier_semaphore()
+    for step in range(1, seq_count):
+        pl.semaphore_signal(
+            barrier,
+            inc=1,
+            device_id=there(lax.rem(seq + step, seq_count)),
+            device_id_type=MESH,
+        )
+    for step in range(1, dp_count):
+        pl.semaphore_signal(
+            barrier,
+            inc=1,
+            device_id={"dp": lax.rem(dp + step, dp_count), "seq": seq},
+            device_id_type=MESH,
+        )
+    pl.semaphore_wait(barrier, seq_count - 1 + dp_count - 1)
+
+    def spread(source_of, target_of, sems, item, target_seq, arrived_at):
+        away = remote(
+            source_of, target_of, sems.at[0, item], sems.at[1, arrived_at], there(target_seq)
+        )
+        here = pltpu.make_async_copy(source_of, target_of, sems.at[1, arrived_at])
+
+        def start():
+            @pl.when(target_seq != seq)
+            def _():
+                away.start()
+
+            @pl.when(target_seq == seq)
+            def _():
+                here.start()
+
+        def wait_sent():
+            @pl.when(target_seq != seq)
+            def _():
+                away.wait_send()
+
+        return start, wait_sent
+
+    def wait_arrived(target, sems, index):
+        pltpu.make_async_copy(target, target, sems.at[1, index]).wait()
+
+    group_of_block = lax.div(seq, half)
+    block_in_group = lax.rem(seq, half)
+    frame_sends = []
+    a0 = layers[0].a
+    for item in range(depth):
+        target = 2 * item + group_of_block
+        frame_sends.append(
+            spread(
+                inputs.frames.at[item],
+                a0.at[at16(16 + 256 * block_in_group, 256)],
+                r.s_frames,
+                item,
+                target,
+                block_in_group,
+            )
+        )
+    for start, _ in frame_sends:
+        start()
+    edge_sems = r.s_frames
+    edge_sends = []
+    for item in range(depth):
+        after = remote(
+            inputs.frames.at[item, pl.ds(248, 8)],
+            a0.at[pl.ds(8, 8)],
+            edge_sems.at[2, item],
+            edge_sems.at[3, 0],
+            there(2 * item + 1),
+        )
+        before = remote(
+            inputs.frames.at[item, pl.ds(0, 8)],
+            a0.at[pl.ds(16 + own_rows[0], 8)],
+            edge_sems.at[2, item],
+            edge_sems.at[3, 0],
+            there(2 * item),
+        )
+        after_here = pltpu.make_async_copy(
+            inputs.frames.at[item, pl.ds(248, 8)], a0.at[pl.ds(8, 8)], edge_sems.at[3, 0]
+        )
+        before_here = pltpu.make_async_copy(
+            inputs.frames.at[item, pl.ds(0, 8)],
+            a0.at[pl.ds(16 + own_rows[0], 8)],
+            edge_sems.at[3, 0],
+        )
+        edge_sends.append((after, before, after_here, before_here, item))
+    sends_after = seq == half - 1
+    sends_before = seq == half
+    for after, before, after_here, before_here, item in edge_sends:
+
+        @pl.when(sends_after & (seq != 2 * item + 1))
+        def _(after=after):
+            after.start()
+
+        @pl.when(sends_after & (seq == 2 * item + 1))
+        def _(after_here=after_here):
+            after_here.start()
+
+        @pl.when(sends_before & (seq != 2 * item))
+        def _(before=before):
+            before.start()
+
+        @pl.when(sends_before & (seq == 2 * item))
+        def _(before_here=before_here):
+            before_here.start()
+
+    def zero_grads(index):
+        r.grads[at8(64 * index, 64), :] = jnp.zeros((64, 256), F32)
+
+    loop(sum(BUCKET_ROWS) // 64, zero_grads)
+    same_group = (
+        lax.broadcasted_iota(jnp.int32, (256, 256), 0) // 32
+        == lax.broadcasted_iota(jnp.int32, (256, 256), 1) // 32
+    )
+    r.gather[...] = jnp.where(same_group, 1.0, 0.0).astype(BF)
+    for copy in time_copies:
+        copy.wait()
+    embedded = mish_of(inputs.flow_embed[pl.ds(place, 1), :])
+    wide_embed = jnp.broadcast_to(embedded, (16, 1024))
+    time_bias = inputs.time_bias[...].astype(F32)
+    for layer in (0, 1):
+        weight = jnp.concatenate([r.half[4 * layer + part] for part in range(4)], 0)
+        projected = dot_weight(wide_embed, weight)
+        r.te[layer] = projected[:8] + time_bias[layer : layer + 1]
+    row16 = lax.broadcasted_iota(jnp.int32, (16, 256), 0)
+    for part in range(4):
+        chosen = jnp.where(
+            row16 == utterance + 64 * member, embedded[:, 256 * part : 256 * part + 256], 0.0
+        )
+        r.grads[pl.ds(EMBED_AT + 16 * part, 16), :] = chosen
+    for copy in weight_copies:
+        copy.wait()
+
+    def valid_rows(start, rows, layer):
+        at = lax.broadcasted_iota(jnp.int32, (rows, 256), 0) + (start - 16)
+        frame = at + member * own_rows[layer]
+        valid = (frame >= 0) & (frame * (1 + layer) < length)
+        return valid, valid & (at >= 0) & (at < own_rows[layer])
+
+    def conv_block(source, start, rows, taps, dims=NN):
+        value = source[at8(start, rows + 16), :]
+        both = jnp.concatenate(split(value), 0)
+        total = None
+        for tap, weight in enumerate(taps):
+            part = dot(both, weight, dims)
+            part = part[: rows + 16] + part[rows + 16 :]
+            part = part[7 + tap : 7 + tap + rows]
+            total = part if total is None else total + part
+        return total
+
+    def send_sums(number):
+        copy = remote(
+            r.sums.at[number],
+            r.sums_in.at[number],
+            r.s_sums.at[0, number],
+            r.s_sums.at[1, number],
+            there(partner),
+        )
+        copy.start()
+        return copy
+
+    def group_total(value):
+        high = value.astype(BF)
+        rest = value - high.astype(F32)
+        middle = rest.astype(BF)
+        last = (rest - middle.astype(F32)).astype(BF)
+        parts = dot(jnp.concatenate([high, middle, last], 0), r.gather[...])
+        total = parts[0:16] + parts[16:32] + parts[32:48]
+        return (
+            jnp.sum(total[0:8], axis=0, keepdims=True),
+            jnp.sum(total[8:16], axis=0, keepdims=True),
+        )
+
+    counts = (
+        (length * 32).astype(F32),
+        (lax.div(length + 1, 2) * 32).astype(F32),
+    )
+
+    def forward_sums(layer, which, copy):
+        number = 2 * layer + which
+        copy.wait()
+        first_sum, second_sum = group_total(r.sums[number] + r.sums_in[number])
+        mean = first_sum / counts[layer]
+        variance = second_sum / counts[layer] - mean * mean
+        r.stat[number, 0:1, :] = mean
+        r.stat[number, 1:2, :] = lax.rsqrt(variance + epsilon)
+
+    def norm_rows(layer, which):
+        number = 2 * layer + which
+        gain = inputs.norm_gain[...].astype(F32)[layer, which : which + 1]
+        bias = inputs.norm_bias[...].astype(F32)[layer, which : which + 1]
+        return r.stat[number, 0:1, :], r.stat[number, 1:2, :], gain, bias
+
+    def add_sums(number, first, second):
+        r.sums[number, 0:8, :] += fold8(first)
+        r.sums[number, 8:16, :] += fold8(second)
+
+    def clear_sums(number):
+        r.sums[number] = jnp.zeros((16, 256), F32)
+
+    def normed_layer(value):
+        mean = jnp.mean(value, axis=1, keepdims=True)
+        centered = value - mean
+        variance = jnp.mean(centered * centered, axis=1, keepdims=True)
+        scale = lax.rsqrt(variance + epsilon)
+        return centered * scale, scale
+
+    def normed_back(grad, normed, scale):
+        return scale * (
+            grad
+            - jnp.mean(grad, axis=1, keepdims=True)
+            - normed * jnp.mean(grad * normed, axis=1, keepdims=True)
+        )
+
+    def layer_rows(layer, which):
+        gain = inputs.layer_gain[...].astype(F32)[layer, which : which + 1]
+        bias = inputs.layer_bias[...].astype(F32)[layer, which : which + 1]
+        return gain, bias
+
+    def row_of(ref, layer):
+        return ref[...].astype(F32)[layer : layer + 1]
+
+    def keys_aux(start, rows, layer):
+        lane = lax.broadcasted_iota(jnp.int32, (rows, 128), 1)
+        key = lax.broadcasted_iota(jnp.int32, (rows, 128), 0) + start
+        masked = jnp.where(key * (1 + layer) < length, 0.0, -1e30)
+        ones = jnp.where((lane >= 65) & (lane < 68), 1.0, 0.0)
+        return jnp.where(lane == 64, masked, ones)
+
+    def both_heads(value):
+        high = value.astype(BF).astype(F32)
+        low = value - high
+        return high, low, pltpu.roll(high, 64, 1), pltpu.roll(low, 64, 1)
+
+    def key_tiles(value, aux):
+        high, low, high_turned, low_turned = both_heads(value)
+        tiles = (
+            (jnp.where(low_half, high, low_turned), jnp.where(low_half, high, aux)),
+            (jnp.where(low_half, high_turned, low), jnp.where(low_half, high_turned, aux)),
+        )
+        return [(a.astype(BF), b.astype(BF)) for a, b in tiles]
+
+    def query_tiles(value, aux):
+        high, low, high_turned, low_turned = both_heads(value)
+        tiles = (
+            (jnp.where(low_half, high, high_turned), jnp.where(low_half, low, aux[0])),
+            (jnp.where(low_half, high_turned, high), jnp.where(low_half, low_turned, aux[1])),
+        )
+        return [(a.astype(BF), b.astype(BF)) for a, b in tiles]
+
+    def three_lanes(value, first):
+        lane = lax.broadcasted_iota(jnp.int32, value.shape, 1)
+        high = value.astype(BF).astype(F32)
+        rest = value - high
+        middle = rest.astype(BF).astype(F32)
+        spread_out = jnp.where(lane == 66, middle, rest - middle)
+        spread_out = jnp.where(lane == 65, high, spread_out)
+        spread_out = jnp.where(lane == 64, first, spread_out)
+        return jnp.where((lane >= 64) & (lane < 68), spread_out, 0.0)
+
+    def res_forward(layer):
+        own = own_rows[layer]
+        extended = own + 16
+        rows = pick(extended, 256)
+        small = pick(extended, 96)
+        a, c1, h, c2 = layers[layer].a, layers[layer].c1, layers[layer].h, layers[layer].c2
+
+        def convolve(source, target, weights, number):
+            clear_sums(number)
+
+            def block(index):
+                out = conv_block(source, rows * index, rows, [weights[layer, k] for k in range(3)])
+                start = rows * index + 8
+                target[at8(start, rows), :] = out
+                kept = jnp.where(valid_rows(start, rows, layer)[1], out, 0.0)
+                add_sums(number, kept, kept * out)
+
+            loop(extended // rows, block)
+            return send_sums(number)
+
+        copy = convolve(a, c1, r.w_conv_one, 2 * layer)
+        forward_sums(layer, 0, copy)
+        mean, scale, gain, bias = norm_rows(layer, 0)
+        added = r.te[layer, 0:1, :]
+
+        def normed(index):
+            start = small * index + 8
+            value = (c1[at8(start, small), :] - mean) * scale * gain + bias
+            valid = valid_rows(start, small, layer)[0]
+            h[at8(start, small), :] = jnp.where(valid, mish_of(value) + added, 0.0)
+
+        loop(extended // small, normed)
+        copy = convolve(h, c2, r.w_conv_two, 2 * layer + 1)
+        forward_sums(layer, 1, copy)
+
+    def kv_copy(layer, index):
+        own = own_rows[layer]
+        part = layers[layer].kv.at[at16(member * own + 256 * index, 256)]
+        return remote(
+            part,
+            part,
+            r.s_kv.at[2 * layer, index],
+            r.s_kv.at[2 * layer + 1, index],
+            there(partner),
+        )
+
+    def qkv_forward(layer):
+        own = own_rows[layer]
+        a, c2, x, kv, qh = layers[layer].a, layers[layer].c2, layers[layer].x, layers[layer].kv, layers[layer].qh
+        mean, scale, gain, bias = norm_rows(layer, 1)
+        layer_gain, layer_bias = layer_rows(layer, 0)
+        lane = lax.broadcasted_iota(jnp.int32, (256, 128), 1)
+        aux = jnp.where(lane == 64, 1.0, 0.0)
+
+        def block(index):
+            start = 256 * index
+            value = (c2[at16(start + 16, 256), :] - mean) * scale * gain + bias
+            valid = valid_rows(start + 16, 256, layer)[0]
+            out = jnp.where(valid, mish_of(value), 0.0)
+            out = out + dot_weight(a[at16(start + 16, 256), :], r.w_res_weight[layer])
+            x[at16(start, 256), :] = out
+            packed = dot_weight(
+                normed_layer(out)[0] * layer_gain + layer_bias, r.w_qkv_weight[layer]
+            )
+            kv[at16(member * own + start, 256), :] = packed[:, 128:]
+            kv_copy(layer, index).start()
+            tiles = query_tiles(packed[:, :128] * (LOG2E / 8.0), (aux, aux))
+            for head in (0, 1):
+                qh[head, at16(start, 256), 0:128] = tiles[head][0]
+                qh[head, at16(start, 256), 128:256] = tiles[head][1]
+
+        loop(own // 256, block)
+
+    def keys_forward(layer):
+        own = own_rows[layer]
+        kv, kh, vh, kt, vt = layers[layer].kv, layers[layer].kh, layers[layer].vh, layers[layer].kt, r.vt
+        for index in range(own // 256):
+            kv_copy(layer, index).wait()
+
+        def block(index):
+            start = 256 * index
+            value = kv[at16(start, 256), :]
+            aux = keys_aux(start, 256, layer)
+            for part, target in ((value[:, :128], kh), (value[:, 128:], vh)):
+                tiles = key_tiles(part, aux)
+                for head in (0, 1):
+                    target[head, at16(start, 256), 0:128] = tiles[head][0]
+                    target[head, at16(start, 256), 128:256] = tiles[head][1]
+            for column in (0, 128):
+                high, low = split(jnp.transpose(value[:, column : column + 128]))
+                for head in (0, 1):
+                    both = jnp.concatenate([high[64 * head : 64 * head + 64], low[64 * head : 64 * head + 64]], 0)
+                    if column == 0:
+                        kt[head, index] = both
+                    else:
+                        vt[head, at16(128 * index, 128), :] = both
+
+        loop(2 * own // 256, block)
+
+    def snake_rows(layer):
+        alpha = jnp.exp(row_of(inputs.snake_alpha, layer))
+        beta = jnp.exp(row_of(inputs.snake_beta, layer))
+        return alpha, beta, 1.0 / (beta + 1e-9)
+
+    def later_forward(layer):
+        own = own_rows[layer]
+        x, att, kh, qh, vt = layers[layer].x, layers[layer].att, layers[layer].kh, layers[layer].qh, r.vt
+        wide, part16 = r.wide, r.half
+        blocks = 2 * own // 256
+        gain, bias = layer_rows(layer, 1)
+        out_bias, down_bias, up_bias = row_of(inputs.out_bias, layer), row_of(inputs.down_bias, layer), row_of(inputs.up_bias, layer)
+        alpha, beta, inverse = snake_rows(layer)
+        turns = alpha * (1.0 / math.pi)
+
+        def block(index):
+            start = 256 * index
+            attended = []
+            for head in (0, 1):
+                query = qh[head, at16(start, 256), :]
+
+                most = jnp.full((8, 256), -3e38, F32)
+                for key in range(blocks):
+                    out = dot(kh[head, 256 * key : 256 * key + 256, :], query, NT)
+                    wide[key] = out
+                    most = jnp.maximum(most, jnp.max(out.reshape(32, 8, 256), axis=0))
+                most = jnp.max(most, axis=0, keepdims=True)
+                total = jnp.zeros((8, 256), F32)
+                for key in range(blocks):
+                    for piece in range(4):
+                        rows = pl.ds(64 * piece, 64)
+                        raised = jnp.exp2(wide[key, rows, :] - most)
+                        total = total + fold8(raised)
+                        high, low = split(raised)
+                        part16[key, rows, :] = high
+                        part16[blocks + key, rows, :] = low
+                total = jnp.sum(total, axis=0, keepdims=True)
+                values = jnp.concatenate([vt[head, 128 * key : 128 * key + 128, :] for key in range(blocks)], 1)
+                out = dot(values, jnp.concatenate([part16[key] for key in range(blocks)], 0))
+                out = out + dot(values, jnp.concatenate([part16[blocks + key] for key in range(blocks)], 0))
+                attended.append((out[:64] + out[64:]) * (1.0 / total))
+                level = jnp.transpose(jnp.broadcast_to(most + jnp.log2(total), (128, 256)))
+                aux = three_lanes(-level, 1.0)
+                old = qh[head, at16(start, 256), 128:256]
+                qh[head, at16(start, 256), 128:256] = jnp.where(low_half, old, aux.astype(BF))
+            joined = jnp.transpose(jnp.concatenate(attended, 0))
+            att[at16(start, 256), :] = joined
+            y = x[at16(start, 256), :] + dot_weight(joined, r.w_out_weight[layer]) + out_bias
+            lifted = dot_weight(normed_layer(y)[0] * gain + bias, r.w_up_weight[layer])
+            for column in range(4):
+                wide[column] = lifted[:, 256 * column : 256 * column + 256]
+            for column in range(4):
+                lanes = slice(256 * column, 256 * column + 256)
+
+                def snake(piece, column=column, lanes=lanes):
+                    rows = pl.ds(64 * piece, 64)
+                    z = wide[column, rows, :] + up_bias[:, lanes]
+                    turn = z * turns[:, lanes]
+                    turn = turn - jnp.round(turn)
+                    square = turn * turn
+                    s = z + square * polynomial(SIN_SQUARE, square) * inverse[:, lanes]
+                    high, low = split(s)
+                    part16[column, rows, :] = high
+                    part16[4 + column, rows, :] = low
+
+                for piece in range(4):
+                    snake(piece)
+            both = jnp.concatenate(
+                [jnp.concatenate([part16[4 * part + column] for column in range(4)], 1) for part in (0, 1)], 0
+            )
+            lowered = dot(both, r.w_down_weight[layer])
+            out = y + lowered[:256] + lowered[256:] + down_bias
+            out = jnp.where(valid_rows(start + 16, 256, layer)[0], out, 0.0)
+            if layer == 0:
+                for lanes in (0, 1):
+                    r.first[lanes, at16(start + 32, 256), :] = out[:, 128 * lanes : 128 * lanes + 128]
+            else:
+                r.last[at16(start, 256), :] = out
+
+        loop(own // 256, block)
+
+    def shrink_forward_part():
+        own = own_rows[0]
+        first = r.first
+        source = pl.multiple_of((1 - member) * (16 + own) + member * 32, 16)
+        target = pl.multiple_of((1 - member) * 16 + member * (32 + own), 16)
+        copy = remote(
+            first.at[:, pl.ds(source, 16), :],
+            first.at[:, pl.ds(target, 16), :],
+            r.s_first.at[0],
+            r.s_first.at[1],
+            there(partner),
+        )
+        copy.start()
+        copy.wait()
+        extended = own_rows[1] + 16
+        rows = pick(extended, 256)
+        bias = inputs.shrink_bias[...].astype(F32).reshape(1, 256)
+
+        def block(index):
+            start = rows * index + 8
+            total = bias
+            for tap in range(3):
+                taken = taken_rows(start - 16, rows, tap)
+                total = total + dot_weight(taken, r.w_shrink_weight[tap])
+            valid = valid_rows(start, rows, 1)[0]
+            layers[1].a[at8(start, rows), :] = jnp.where(valid, total, 0.0)
+
+        loop(extended // rows, block)
+
+    def taken_rows(row, rows, tap):
+        at = 32 + 2 * row - 1 + tap
+        return jnp.concatenate([r.first[lanes, pl.ds(at, rows, stride=2), :] for lanes in (0, 1)], 1)
+
+    def clear_layer():
+        r.narrow_acc[...] = jnp.zeros((8, 8, 256), F32)
+        r.wide_acc[...] = jnp.zeros((3, 8, 1024), F32)
+
+    def later_backward(layer, advances={}):
+        own = own_rows[layer]
+        base = LATER_AT[layer]
+        x, att, qh = layers[layer].x, layers[layer].att, layers[layer].qh
+        wide, part16, grads = r.wide, r.half, r.grads
+        doh = r.vt
+        gain, bias = layer_rows(layer, 1)
+        out_bias, up_bias = row_of(inputs.out_bias, layer), row_of(inputs.up_bias, layer)
+        alpha, beta, inverse = snake_rows(layer)
+        turns = alpha * (1.0 / math.pi)
+        slope = alpha * inverse
+        r.tall[...] = jnp.zeros((256, 1024), F32)
+        clear_layer()
+        narrow, broad = r.narrow_acc, r.wide_acc
+
+        def block(index):
+            start = 256 * index
+            if layer == 0:
+                dout = jnp.concatenate([r.dfirst[lanes, at16(start, 256), :] for lanes in (0, 1)], 1)
+            else:
+                dout = r.cot[at16(start, 256), :]
+            joined = att[at16(start, 256), :]
+            y = x[at16(start, 256), :] + dot_weight(joined, r.w_out_weight[layer]) + out_bias
+            normed, scale = normed_layer(y)
+            entered = normed * gain + bias
+            lifted = dot_weight(entered, r.w_up_weight[layer])
+            for column in range(4):
+                wide[column] = lifted[:, 256 * column : 256 * column + 256]
+            risen = dot_weight(dout, r.w_down_weight[layer], NT)
+            for column in range(4):
+                wide[4 + column] = risen[:, 256 * column : 256 * column + 256]
+            for column in range(4):
+                lanes = slice(256 * column, 256 * column + 256)
+
+                dz_sum = turn_sum = sine_sum = jnp.zeros((8, 256), F32)
+                for piece in range(8):
+                    rows = pl.ds(32 * piece, 32)
+                    z = wide[column, rows, :] + up_bias[:, lanes]
+                    ds = wide[4 + column, rows, :]
+                    whole = z * turns[:, lanes]
+                    turn = whole - jnp.round(whole)
+                    square = turn * turn
+                    sine2 = square * polynomial(SIN_SQUARE, square)
+                    twice = turn * polynomial(SIN_TWICE, square)
+                    s = z + sine2 * inverse[:, lanes]
+                    dtwice = ds * twice
+                    dz = ds + dtwice * slope[:, lanes]
+                    dz_sum += fold8(dz)
+                    turn_sum += fold8(dtwice * whole)
+                    sine_sum += fold8(ds * sine2)
+                    high, low = split(s)
+                    part16[column, rows, :] = high
+                    part16[4 + column, rows, :] = low
+                    high, low = split(dz)
+                    part16[8 + column, rows, :] = high
+                    part16[12 + column, rows, :] = low
+                broad[0, :, lanes] += dz_sum
+                broad[1, :, lanes] += turn_sum
+                broad[2, :, lanes] += sine_sum
+
+            def gathered(number):
+                return jnp.concatenate([part16[number + column] for column in range(4)], 1)
+
+            r.tall[...] += dot_pair(split(jnp.transpose(dout)), (gathered(0), gathered(4)))
+            raised = dot_pair(split(jnp.transpose(entered)), (gathered(8), gathered(12)))
+            for column in range(4):
+                grads[pl.ds(base + UP + 256 * column, 256), :] += raised[:, 256 * column : 256 * column + 256]
+            both = dot(jnp.concatenate([gathered(8), gathered(12)], 0), r.w_up_weight[layer], NT)
+            dentered = both[:256] + both[256:]
+            dy = dout + normed_back(dentered * gain, normed, scale)
+            r.dy[at16(start, 256), :] = dy
+            narrow[0] += fold8(dout)
+            narrow[1] += fold8(dy)
+            narrow[2] += fold8(dentered * normed)
+            narrow[3] += fold8(dentered)
+            grads[pl.ds(base + OUT, 128), :] += dot_pair(split(jnp.transpose(joined)), split(dy))
+            datt = dot_weight(dy, r.w_out_weight[layer], NT)
+            product = datt * joined
+            sums = [
+                jnp.sum(jnp.where(low_half, product, 0.0), axis=1, keepdims=True),
+                jnp.sum(jnp.where(low_half, 0.0, product), axis=1, keepdims=True),
+            ]
+            aux = [three_lanes(jnp.broadcast_to(-total, (256, 128)), 0.0) for total in sums]
+            tiles = query_tiles(datt, aux)
+            pairs = key_tiles(datt, aux[0])
+            for head in (0, 1):
+                doh[head, at16(start, 256), 0:128] = tiles[head][0]
+                doh[head, at16(start, 256), 128:256] = tiles[head][1]
+                r.dd[head, at16(start, 256), :] = pairs[head][0]
+                query = qh[head, at16(start, 256), 0:128].astype(F32)
+                rest = pltpu.roll(qh[head, at16(start, 256), 128:256].astype(F32), 64, 1)
+                r.qq[head, at16(start, 256), :] = jnp.where(low_half, query, rest).astype(BF)
+
+        loop_with(own // 256, block, advances)
+
+        def turn_down(index):
+            taken = r.tall[:, pl.ds(pl.multiple_of(256 * index, 256), 256)]
+            grads[at16(base + DOWN + 256 * index, 256), :] = jnp.transpose(taken)
+
+        loop(4, turn_down)
+        small = base + LATER_SMALL
+        for number in range(4):
+            grads[pl.ds(small + number, 1), :] = jnp.sum(narrow[number], axis=0, keepdims=True)
+        bias_row = jnp.sum(broad[0], axis=0, keepdims=True)
+        alpha_row = jnp.sum(broad[1], axis=0, keepdims=True) * (math.pi * inverse)
+        beta_row = jnp.sum(broad[2], axis=0, keepdims=True) * (-beta * inverse * inverse)
+        for number, row in enumerate((bias_row, alpha_row, beta_row)):
+            for column in range(4):
+                grads[pl.ds(small + 4 + 4 * number + column, 1), :] = row[:, 256 * column : 256 * column + 256]
+
+    def dk_copy(layer):
+        own = own_rows[layer]
+        return remote(
+            layers[layer].kv.at[at16((1 - member) * own, own)],
+            r.dkr.at[pl.ds(0, own)],
+            r.s_dk.at[2 * layer],
+            r.s_dk.at[2 * layer + 1],
+            there(partner),
+        )
+
+    def attend_backward(layer, advances={}, more={}):
+        own = own_rows[layer]
+        kh, vh, qh, kt, dkv = layers[layer].kh, layers[layer].vh, layers[layer].qh, layers[layer].kt, layers[layer].kv
+        doh, dd, qq, part16 = r.vt, r.dd, r.qq, r.half
+        blocks, queries = 2 * own // 256, own // 256
+        for head in (0, 1):
+            r.tall[pl.ds(128 * head, 128), 0:own] = jnp.zeros((128, own), F32)
+
+        def block(index):
+            key = lax.rem((1 - member) * queries + index, blocks)
+            found = []
+            for head in (0, 1):
+                keys = kh[head, at16(256 * key, 256), :]
+                values = vh[head, at16(256 * key, 256), :]
+                for query in range(queries):
+                    rows = pl.ds(256 * query, 256)
+                    weights = jnp.exp2(dot(keys, qh[head, rows, :], NT))
+                    grad = weights * dot(values, doh[head, rows, :], NT)
+                    high, low = split(weights)
+                    part16[query] = high
+                    part16[4 + query] = low
+                    high, low = split(grad)
+                    part16[8 + query] = high
+                    part16[12 + query] = low
+
+                def gathered(number):
+                    return jnp.concatenate([part16[number + query] for query in range(queries)], 1)
+
+                dscores, dscores_rest = gathered(8), gathered(12)
+                both = dot(jnp.concatenate([gathered(0), gathered(4)], 0), dd[head, 0:own, :])
+                dvalue = both[:256] + both[256:]
+                both = dot(jnp.concatenate([dscores, dscores_rest], 0), qq[head, 0:own, :])
+                dkey = both[:256] + both[256:]
+                found.append((dkey, dvalue))
+                r.tall[pl.ds(128 * head, 128), 0:own] += dot(kt[head, key], dscores) + dot(kt[head, key], dscores_rest)
+            for column, part in ((0, 0), (128, 1)):
+                zeroth = found[0][part] + pltpu.roll(found[0][part], 64, 1)
+                other = found[1][part] + pltpu.roll(found[1][part], 64, 1)
+                joined = jnp.where(low_half, zeroth, other)
+                if part == 0:
+                    joined = joined * LN2
+                dkv[at16(256 * key, 256), column : column + 128] = joined
+
+        loop_with(queries, block, advances)
+        copy = dk_copy(layer)
+        copy.start()
+        loop_with(queries, lambda index: block(index + queries), more)
+        copy.wait()
+
+    def qkv_backward(layer, advances={}):
+        own = own_rows[layer]
+        x, c2, dkv, dkr = layers[layer].x, layers[layer].c2, layers[layer].kv, r.dkr
+        grads, narrow = r.grads, r.narrow_acc
+        gain, bias = layer_rows(layer, 0)
+        mean2, scale2, gain2, bias2 = norm_rows(layer, 1)
+        number = 4 + 2 * layer
+        clear_sums(number)
+
+        def block(index):
+            start = 256 * index
+            lanes = pl.ds(pl.multiple_of(start, 256), 256)
+            dquery = [r.tall[pl.ds(128 * head, 64), lanes] + r.tall[pl.ds(128 * head + 64, 64), lanes] for head in (0, 1)]
+            dquery = jnp.transpose(jnp.concatenate(dquery, 0)) * 0.125
+            dkeys = dkv[at16(member * own + start, 256), :] + dkr[at16(start, 256), :]
+            packed = jnp.concatenate([dquery, dkeys], 1)
+            normed, scale = normed_layer(x[at16(start, 256), :])
+            entered = normed * gain + bias
+            weight = dot_pair(split(jnp.transpose(entered)), split(packed))
+            grads[pl.ds(QUERY_KEY_AT[layer], 256), :] += weight[:, :256]
+            grads[pl.ds(VALUE_AT[layer], 128), 0:128] += weight[:128, 256:]
+            grads[pl.ds(VALUE_AT[layer], 128), 128:256] += weight[128:, 256:]
+            dentered = dot_weight(packed, r.w_qkv_weight[layer], NT)
+            narrow[4] += fold8(dentered * normed)
+            narrow[5] += fold8(dentered)
+            dx = r.dy[at16(start, 256), :] + normed_back(dentered * gain, normed, scale)
+            r.dx[at16(start + 16, 256), :] = dx
+            unit = (c2[at16(start + 16, 256), :] - mean2) * scale2
+            dvalue = dx * mish_slope(unit * gain2 + bias2)
+            add_sums(number, dvalue, dvalue * unit)
+
+        loop_with(own // 256, block, advances)
+        for row in (4, 5):
+            grads[pl.ds(SMALL_AT[layer] + row, 1), :] = jnp.sum(narrow[row], axis=0, keepdims=True)
+        copy = send_sums(number)
+        source = pl.multiple_of((1 - member) * (8 + own) + member * 16, 8)
+        target = pl.multiple_of((1 - member) * 8 + member * (16 + own), 8)
+        edge = remote(
+            r.dx.at[pl.ds(source, 8)],
+            r.dx.at[pl.ds(target, 8)],
+            r.s_dx.at[2 * layer],
+            r.s_dx.at[2 * layer + 1],
+            there(partner),
+        )
+        edge.start()
+        return copy, edge
+
+    def norm_back(layer, which, copy):
+        number = 4 + 2 * layer + (1 - which)
+        base = SMALL_AT[layer]
+        copy.wait()
+        mean, scale, gain, bias = norm_rows(layer, which)
+        mine = r.sums[number]
+        r.grads[pl.ds(base + 2 + which, 1), :] = jnp.sum(mine[0:8], axis=0, keepdims=True)
+        r.grads[pl.ds(base + which, 1), :] = jnp.sum(mine[8:16], axis=0, keepdims=True)
+        from_bias, from_gain = group_total((mine + r.sums_in[number]) * gain)
+        return mean, scale, gain, bias, from_bias / counts[layer], from_gain / counts[layer]
+
+    def weight_rows(at, taken, grad):
+        left = [split(jnp.transpose(value)) for value in taken]
+        high = jnp.concatenate([pair[0] for pair in left], 0)
+        low = jnp.concatenate([pair[1] for pair in left], 0)
+        r.grads[pl.ds(at, 256 * len(taken)), :] += dot_pair((high, low), split(grad))
+
+    def conv_weight(source, target, own, at):
+        def block(index):
+            value = source[at8(256 * index + 8, 272), :]
+            grad = target[at16(256 * index + 16, 256), :]
+            weight_rows(at, [value[7 + tap : 263 + tap] for tap in range(3)], grad)
+
+        loop(own // 256, block)
+
+    def res_backward(layer, copies, advances=((), ())):
+        own = own_rows[layer]
+        extended = own + 16
+        rows, small = pick(extended, 256), pick(extended, 96)
+        a, c1, h, c2 = layers[layer].a, layers[layer].c1, layers[layer].h, layers[layer].c2
+        dx, dv = r.dx, layers[0].kv
+        copy, edge = copies
+        edge.wait()
+        zero(dv, 0, 16)
+        zero(dv, own + 16, 16)
+        mean, scale, gain, bias, from_bias, from_gain = norm_back(layer, 1, copy)
+
+        def second(index):
+            start = small * index + 8
+            unit = (c2[at8(start, small), :] - mean) * scale
+            grad = dx[at8(start, small), :] * mish_slope(unit * gain + bias)
+            out = scale * (gain * grad - (from_bias + unit * from_gain))
+            c2[at8(start, small), :] = jnp.where(valid_rows(start, small, layer)[0], out, 0.0)
+
+        loop(extended // small, second)
+        mean1, scale1, gain1, bias1 = norm_rows(layer, 0)
+        number = 5 + 2 * layer
+        clear_sums(number)
+        r.narrow_acc[6] = jnp.zeros((8, 256), F32)
+
+        def hidden(index):
+            start = rows * index + 8
+            taps = [r.w_conv_two[layer, 2 - tap] for tap in range(3)]
+            out = conv_block(c2, rows * index, rows, taps, NT)
+            valid, mine = valid_rows(start, rows, layer)
+            out = jnp.where(valid, out, 0.0)
+            unit = (c1[at8(start, rows), :] - mean1) * scale1
+            grad = out * mish_slope(unit * gain1 + bias1)
+            dv[at8(start, rows), :] = grad
+            r.narrow_acc[6] += fold8(jnp.where(mine, out, 0.0))
+            grad = jnp.where(mine, grad, 0.0)
+            add_sums(number, grad, grad * unit)
+
+        loop(extended // rows, hidden)
+        copy = send_sums(number)
+        conv_weight(h, c2, own, CONV_TWO_AT[layer])
+
+        def res_part(index):
+            value = a[at16(256 * index + 16, 256), :]
+            weight_rows(RES_AT[layer], [value], dx[at16(256 * index + 16, 256), :])
+
+        loop(own // 256, res_part)
+        advance(*advances[0])
+        summed = jnp.sum(r.narrow_acc[6], axis=0, keepdims=True)
+        r.grads[pl.ds(SMALL_AT[layer] + 8, 16), :] = jnp.where(row16 == utterance, summed, 0.0)
+        mean, scale, gain, bias, from_bias, from_gain = norm_back(layer, 0, copy)
+
+        def first_part(index):
+            start = small * index + 8
+            unit = (c1[at8(start, small), :] - mean) * scale
+            out = scale * (gain * dv[at8(start, small), :] - (from_bias + unit * from_gain))
+            dv[at8(start, small), :] = jnp.where(valid_rows(start, small, layer)[0], out, 0.0)
+
+        loop(extended // small, first_part)
+        taps = [r.w_conv_one[layer, 2 - tap] for tap in range(3)]
+
+        def inputs(start, size):
+            out = conv_block(dv, start, size, taps, NT)
+            out = out + dot_weight(dx[at8(start + 8, size), :], r.w_res_weight[layer], NT)
+            return jnp.where(valid_rows(start + 8, size, layer)[0], out, 0.0)
+
+        if layer == 1:
+
+            def block(index):
+                r.da[at8(rows * index + 8, rows), :] = inputs(rows * index, rows)
+
+            loop(extended // rows, block)
+        else:
+
+            def block(index):
+                r.dy[at16(256 * index, 256), :] = inputs(256 * index + 8, 256)
+
+            loop(own // 256, block)
+            send_blocks(r.dy, 256, input_grad, r.s_grad)
+        advance(*advances[1])
+        conv_weight(a, dv, own, CONV_ONE_AT[layer])
+
+    def shrink_backward_part():
+        da, own = r.da, own_rows[1]
+        acc = r.narrow_acc
+        acc[7] = jnp.zeros((8, 256), F32)
+
+        def block(index):
+            value = da[at16(128 * index + 16, 144), :]
+            both = jnp.concatenate(split(value), 0)
+            parts = [dot(both, r.w_shrink_weight[tap], NT) for tap in range(3)]
+            parts = [part[:144] + part[144:] for part in parts]
+            even = parts[1][:128]
+            odd = parts[2][:128] + parts[0][1:129]
+            at = lax.broadcasted_iota(jnp.int32, (128, 256), 0) + 128 * index
+            frame = 2 * (at + member * own)
+            even = jnp.where(frame < length, even, 0.0)
+            odd = jnp.where(frame + 1 < length, odd, 0.0)
+            for lanes in (0, 1):
+                columns = slice(128 * lanes, 128 * lanes + 128)
+                r.dfirst[lanes, pl.ds(256 * index, 128, stride=2), :] = even[:, columns]
+                r.dfirst[lanes, pl.ds(256 * index + 1, 128, stride=2), :] = odd[:, columns]
+            acc[7] += fold8(value[:128])
+
+        loop(own // 128, block)
+
+        def weights(index):
+            grad = da[at16(256 * index + 16, 256), :]
+            weight_rows(SHRINK_AT, [taken_rows(256 * index, 256, tap) for tap in range(3)], grad)
+
+        loop(own // 256, weights)
+        r.grads[pl.ds(SMALL_AT[1] + 6, 1), :] = jnp.sum(acc[7], axis=0, keepdims=True)
+
+    def block_sends(source, size, target, sems):
+        return [
+            spread(
+                source.at[pl.ds(size * item, size)],
+                target.at[place],
+                sems,
+                item,
+                half * member + item,
+                place,
+            )
+            for item in range(half)
+        ]
+
+    def send_blocks(source, size, target, sems):
+        for start, _ in block_sends(source, size, target, sems):
+            start()
+
+    def finish_blocks(source, size, target, sems):
+        for _, wait_sent in block_sends(source, size, target, sems):
+            wait_sent()
+        for item in range(depth):
+            wait_arrived(target.at[item], sems, item)
+
+    def bucket(number):
+        grads, sems, arrived = r.grads, r.s_total, arrivals[number]
+        size = BUCKET_ROWS[number]
+        first = size // 512 * 256
+        if first == 0:
+            first = size
+        x, y = lax.rem(dp, 2), lax.div(dp, 2)
+        over_x, over_y = (x, dp + 1 - 2 * x), (y, dp + 2 - 4 * y)
+        lanes = []
+        for at, count, order in (
+            (BUCKET_AT[number], size - first, (over_x, over_y)),
+            (BUCKET_AT[number] + size - first, first, (over_y, over_x)),
+        ):
+            if count == 0:
+                continue
+            size1, size2, size3, size4 = count // 2, count // 4, count // 8, count // (8 * depth)
+            start1 = at + member * size1
+            start2 = start1 + order[0][0] * size2
+            start3 = start2 + order[1][0] * size3
+            start4 = start3 + place * size4
+            lanes.append(
+                (
+                    (at + (1 - member) * size1, start1, size1, there(partner)),
+                    (
+                        start1 + (1 - order[0][0]) * size2,
+                        start2,
+                        size2,
+                        {"dp": order[0][1], "seq": seq},
+                    ),
+                    (
+                        start2 + (1 - order[1][0]) * size3,
+                        start3,
+                        size3,
+                        {"dp": order[1][1], "seq": seq},
+                    ),
+                    (start3, start4, size4),
+                )
+            )
+
+        def rows_at(ref, start, count):
+            return ref.at[at8(start, count)]
+
+        def wait_bytes(count, sem):
+            some = rows_at(grads, BUCKET_AT[number], count)
+            pltpu.make_async_copy(some, some, sem).wait()
+
+        def total_of(stage):
+            return sum(lane[stage][2] for lane in lanes)
+
+        def arriving(stage):
+            if stage == 0:
+                return r.core, CORE_AT[number]
+            return (arrived.near, arrived.next)[stage - 1], 0
+
+        def pair_out(stage):
+            into, at = arriving(stage)
+            for lane in lanes:
+                given, _, count, device = lane[stage]
+                remote(
+                    rows_at(grads, given, count),
+                    into.at[pl.ds(at, count)],
+                    sems.at[number, 2 * stage],
+                    sems.at[number, 2 * stage + 1],
+                    device,
+                ).start()
+                at += count
+
+        def pair_in(stage):
+            wait_bytes(total_of(stage), sems.at[number, 2 * stage])
+            wait_bytes(total_of(stage), sems.at[number, 2 * stage + 1])
+            into, at = arriving(stage)
+            for lane in lanes:
+                _, start, count, _ = lane[stage]
+                add_all(start, count, [into.at[pl.ds(at, count)]])
+                at += count
+
+        def far_peers():
+            for step in range(1, depth):
+                yield step, lax.rem(place + step, depth)
+
+        def far_out():
+            at = 0
+            for lane in lanes:
+                start3, _, count = lane[3]
+                for step, other in far_peers():
+                    remote(
+                        rows_at(grads, start3 + other * count, count),
+                        arrived.far.at[step - 1, pl.ds(at, count)],
+                        sems.at[number, 6],
+                        sems.at[number, 7],
+                        there(2 * other + member),
+                    ).start()
+                at += count
+
+        def far_in():
+            wait_bytes(total_of(3) * (depth - 1), sems.at[number, 6])
+            wait_bytes(total_of(3) * (depth - 1), sems.at[number, 7])
+            at = 0
+            for lane in lanes:
+                _, start4, count = lane[3]
+                parts = [arrived.far.at[step, pl.ds(at, count)] for step in range(depth - 1)]
+                add_all(start4, count, parts)
+                at += count
+
+        def far_back():
+            for lane in lanes:
+                _, start4, count = lane[3]
+                for _, other in far_peers():
+                    remote(
+                        rows_at(grads, start4, count),
+                        rows_at(grad_total, start4, count),
+                        sems.at[number, 8],
+                        sems.at[number, 9],
+                        there(2 * other + member),
+                    ).start()
+                pltpu.make_async_copy(
+                    rows_at(grads, start4, count),
+                    rows_at(grad_total, start4, count),
+                    sems.at[number, 16],
+                ).start()
+
+        def far_back_in():
+            wait_bytes(total_of(3) * (depth - 1), sems.at[number, 8])
+            wait_bytes(total_of(3) * (depth - 1), sems.at[number, 9])
+            wait_bytes(total_of(3), sems.at[number, 16])
+
+        def pair_back(stage):
+            for lane in lanes:
+                _, start, count, device = lane[stage]
+                remote(
+                    rows_at(grad_total, start, count),
+                    rows_at(grad_total, start, count),
+                    sems.at[number, 14 - 2 * stage],
+                    sems.at[number, 15 - 2 * stage],
+                    device,
+                ).start()
+
+        def pair_back_in(stage):
+            wait_bytes(total_of(stage), sems.at[number, 14 - 2 * stage])
+            wait_bytes(total_of(stage), sems.at[number, 15 - 2 * stage])
+
+        def add_all(start, count, parts):
+            unit = pick8(count, 64)
+
+            def piece(index):
+                rows = at8(start + unit * index, unit)
+                value = grads[rows, :]
+                for part in parts:
+                    value = value + part[at8(unit * index, unit), :]
+                grads[rows, :] = value
+
+            loop(count // unit, piece)
+
+        def step(which):
+            if which in (1, 2, 3):
+                pair_in(which - 1)
+            if which == 4:
+                far_in()
+            if which == 5:
+                far_back_in()
+            if which in (6, 7, 8):
+                pair_back_in(8 - which)
+            if which in (0, 1, 2):
+                pair_out(which)
+            if which == 3:
+                far_out()
+            if which == 4:
+                far_back()
+            if which in (5, 6, 7):
+                pair_back(7 - which)
+
+        return step
+
+    all_steps = [bucket(number) for number in range(len(BUCKET_ROWS))]
+
+    def advance(*pairs):
+        for number, which in pairs:
+            all_steps[number](which)
+
+    def loop_with(count, body, advances):
+        def step(index):
+            for at, pairs in advances.items():
+
+                @pl.when(index == at)
+                def _(pairs=pairs):
+                    advance(*pairs)
+
+            body(index)
+
+        loop(count, step)
+
+    for item in range(depth):
+        wait_arrived(a0.at[pl.ds(16 + 256 * item, 256)], r.s_frames, item)
+    pltpu.make_async_copy(a0.at[pl.ds(8, 8)], a0.at[pl.ds(8, 8)], edge_sems.at[3, 0]).wait()
+
+    def mask_frames(index):
+        rows = at8(pick(own_rows[0] + 16, 96) * index + 8, pick(own_rows[0] + 16, 96))
+        valid = valid_rows(pick(own_rows[0] + 16, 96) * index + 8, pick(own_rows[0] + 16, 96), 0)[0]
+        a0[rows, :] = jnp.where(valid, a0[rows, :], 0.0)
+
+    loop((own_rows[0] + 16) // pick(own_rows[0] + 16, 96), mask_frames)
+    cot_sends = [
+        spread(
+            inputs.cotangent.at[item],
+            r.cot.at[at16(128 * block_in_group, 128)],
+            r.s_cot,
+            item,
+            2 * item + group_of_block,
+            block_in_group,
+        )
+        for item in range(depth)
+    ]
+    for start, _ in cot_sends:
+        start()
+    res_forward(0)
+    qkv_forward(0)
+    keys_forward(0)
+    later_forward(0)
+    shrink_forward_part()
+    res_forward(1)
+    qkv_forward(1)
+    keys_forward(1)
+    later_forward(1)
+    send_blocks(r.last, 128, output, r.s_last)
+    for item in range(depth):
+        wait_arrived(r.cot.at[pl.ds(128 * item, 128)], r.s_cot, item)
+
+    def mask_cot(index):
+        valid = valid_rows(128 * index + 16, 128, 1)[0]
+        rows = at16(128 * index, 128)
+        r.cot[rows, :] = jnp.where(valid, r.cot[rows, :], 0.0)
+
+    loop(own_rows[1] // 128, mask_cot)
+    later_backward(1)
+    advance((0, 0))
+    attend_backward(1)
+    advance((0, 1))
+    copies = qkv_backward(1)
+    res_backward(1, copies)
+    shrink_backward_part()
+    advance((0, 2), (1, 0))
+    later_backward(0, {1: [(0, 3), (1, 1)], 3: [(0, 4), (1, 2)]})
+    advance((2, 0))
+    attend_backward(0, {1: [(1, 3)], 2: [(0, 5), (2, 1)]}, {0: [(0, 6)], 2: [(1, 4), (2, 2)]})
+    advance((0, 7))
+    copies = qkv_backward(0, {2: [(2, 3)]})
+    advance((1, 5))
+    res_backward(0, copies, [[(3, 0)], [(2, 4), (1, 6), (3, 1)]])
+    advance((4, 0), (3, 2), (4, 1), (2, 5), (3, 3), (4, 2), (1, 7), (0, 8), (2, 6))
+    advance((4, 3), (3, 4), (4, 4), (3, 5), (2, 7), (1, 8), (4, 5), (3, 6), (2, 8), (4, 6), (3, 7), (4, 7), (3, 8), (4, 8))
+    for _, wait_sent in frame_sends + cot_sends:
+        wait_sent()
+    for after, before, _, _, item in edge_sends:
+
+        @pl.when(sends_after & (seq != 2 * item + 1))
+        def _(after=after):
+            after.wait_send()
+
+        @pl.when(sends_before & (seq != 2 * item))
+        def _(before=before):
+            before.wait_send()
+
+    finish_blocks(r.last, 128, output, r.s_last)
+    finish_blocks(r.dy, 256, input_grad, r.s_grad)
+
+
+def pick8(total, most):
+    best = 8
+    for size in range(8, most + 1, 8):
+        if total % size == 0:
+            best = size
+    return best
+
+
+GRAD_SHAPES = (
+    (2, 3, 256, 256),
+    (2, 3, 256, 256),
+    (2, 256, 256),
+    (2, 2, 256),
+    (2, 2, 256),
+    (2, 1024, 256),
+    (2, 256),
+    (2, 2, 256),
+    (2, 2, 256),
+    (2, 256, 384),
+    (2, 128, 256),
+    (2, 256),
+    (2, 256, 1024),
+    (2, 1024),
+    (2, 1024),
+    (2, 1024),
+    (2, 1024, 256),
+    (2, 256),
+    (3, 256, 256),
+    (256,),
+)
+
+class Gradients(typing.NamedTuple):
+    conv_one: Any
+    conv_two: Any
+    res_weight: Any
+    norm_gain: Any
+    norm_bias: Any
+    time_weight: Any
+    time_bias: Any
+    layer_gain: Any
+    layer_bias: Any
+    qkv_weight: Any
+    out_weight: Any
+    out_bias: Any
+    up_weight: Any
+    up_bias: Any
+    snake_alpha: Any
+    snake_beta: Any
+    down_weight: Any
+    down_bias: Any
+    shrink_weight: Any
+    shrink_bias: Any
+
+
+def unpack_kernel(shape, total, *refs):
+    outs = Gradients(*refs[:20])
+    held, sems, out_sems = refs[20:]
+    loads, stores = [], []
+
+    def rows(start, count):
+        return total.at[pl.ds(start, count)], held.at[pl.ds(start, count)]
+
+    def load(start, count):
+        source, target = rows(start, count)
+        loads.append(pltpu.make_async_copy(source, target, sems.at[len(loads)]))
+        loads[-1].start()
+
+    def store(start, count, target, lanes=pl.ds(0, 256)):
+        source = held.at[pl.ds(start, count), lanes]
+        stores.append((pltpu.make_async_copy(source, target, out_sems.at[len(stores)]), len(loads)))
+
+    def move(start, count, target):
+        load(start, count)
+        store(start, count, target)
+
+    for layer in (1, 0):
+        later = LATER_AT[layer]
+        for column in range(4):
+            lanes = pl.ds(256 * column, 256)
+            move(later + UP + 256 * column, 256, outs.up_weight.at[layer, :, lanes])
+        move(later + DOWN, 1024, outs.down_weight.at[layer])
+        move(later + OUT, 128, outs.out_weight.at[layer])
+        load(later + LATER_SMALL, 16)
+        for tap in range(3):
+            move(CONV_TWO_AT[layer] + 256 * tap, 256, outs.conv_two.at[layer, tap])
+        move(RES_AT[layer], 256, outs.res_weight.at[layer])
+        move(QUERY_KEY_AT[layer], 256, outs.qkv_weight.at[layer, :, pl.ds(0, 256)])
+        for tap in range(3):
+            move(CONV_ONE_AT[layer] + 256 * tap, 256, outs.conv_one.at[layer, tap])
+        load(VALUE_AT[layer], 128)
+        for part in (0, 1):
+            target = outs.qkv_weight.at[layer, pl.ds(128 * part, 128), pl.ds(256, 128)]
+            store(VALUE_AT[layer], 128, target, pl.ds(128 * part, 128))
+        load(SMALL_AT[layer], 24)
+    for tap in range(3):
+        move(SHRINK_AT + 256 * tap, 256, outs.shrink_weight.at[tap])
+    load(EMBED_AT, 64)
+    waited = 0
+    for copy, needed in stores:
+        for number in range(waited, needed):
+            loads[number].wait()
+        waited = needed
+        copy.start()
+    for number in range(waited, len(loads)):
+        loads[number].wait()
+    for layer in (0, 1):
+        later = held[pl.ds(LATER_AT[layer] + LATER_SMALL, 16), :]
+        res = held[pl.ds(SMALL_AT[layer], 24), :]
+        outs.norm_gain[layer] = res[0:2]
+        outs.norm_bias[layer] = res[2:4]
+        outs.layer_gain[layer, 0:1, :] = res[4:5]
+        outs.layer_gain[layer, 1:2, :] = later[2:3]
+        outs.layer_bias[layer, 0:1, :] = res[5:6]
+        outs.layer_bias[layer, 1:2, :] = later[3:4]
+        outs.down_bias[layer : layer + 1, :] = later[0:1]
+        outs.out_bias[layer : layer + 1, :] = later[1:2]
+        for column in range(4):
+            lanes = slice(256 * column, 256 * column + 256)
+            outs.up_bias[layer : layer + 1, lanes] = later[4 + column : 5 + column]
+            outs.snake_alpha[layer : layer + 1, lanes] = later[8 + column : 9 + column]
+            outs.snake_beta[layer : layer + 1, lanes] = later[12 + column : 13 + column]
+        summed = res[8:24]
+        outs.time_bias[layer : layer + 1, :] = jnp.sum(summed, axis=0, keepdims=True)
+        right = split(summed)
+        blank = jnp.zeros((128 - 16, 256), F32)
+        for column in range(4):
+            tall = jnp.concatenate([held[pl.ds(EMBED_AT + 16 * column, 16), :], blank], 0)
+            left = split(jnp.transpose(tall)[:, 0:16])
+            outs.time_weight[layer, pl.ds(256 * column, 256), :] = dot_pair(left, right)
+    outs.shrink_bias[...] = held[pl.ds(SMALL_AT[1] + 6, 1), :]
+    for copy, _ in stores:
+        copy.wait()
+
+
+def fused_local(shape, *args):
+    groups = scratch_of(shape)
+    given = Arguments(*args)
+    specs = Arguments(*(WHOLE,) * 24)._replace(
+        frames=ANY,
+        lengths=pl.BlockSpec(memory_space=pltpu.SMEM),
+        cotangent=ANY,
+        conv_one=ANY,
+        conv_two=ANY,
+        res_weight=ANY,
+        time_weight=ANY,
+        qkv_weight=ANY,
+        out_weight=ANY,
+        up_weight=ANY,
+        down_weight=ANY,
+        shrink_weight=ANY,
+    )
+    output, input_grad, total = pl.pallas_call(
+        lambda *refs: fused_kernel(shape, groups, *refs),
+        out_shape=(
+            jax.ShapeDtypeStruct(given.cotangent.shape, F32),
+            jax.ShapeDtypeStruct(given.frames.shape, F32),
+            jax.ShapeDtypeStruct((sum(BUCKET_ROWS), 256), F32),
+        ),
+        in_specs=list(specs),
+        out_specs=(ANY,) * 3,
+        scratch_shapes=[one for group in groups for one in group.values()],
+        name="layers",
+        compiler_params=pltpu.CompilerParams(
+            collective_id=0, has_side_effects=True, vmem_limit_bytes=VMEM_BYTES
+        ),
+    )(*given)
+    shapes = [s if len(s) > 1 else (1,) + s for s in GRAD_SHAPES]
+    grads = pl.pallas_call(
+        lambda *refs: unpack_kernel(shape, *refs),
+        out_shape=tuple(jax.ShapeDtypeStruct(s, F32) for s in shapes),
+        in_specs=[ANY],
+        out_specs=tuple(
+            Gradients(*(WHOLE,) * 20)._replace(
+                conv_one=ANY,
+                conv_two=ANY,
+                res_weight=ANY,
+                qkv_weight=ANY,
+                out_weight=ANY,
+                up_weight=ANY,
+                down_weight=ANY,
+                shrink_weight=ANY,
+            )
+        ),
+        scratch_shapes=[
+            pltpu.VMEM((sum(BUCKET_ROWS), 256), F32),
+            pltpu.SemaphoreType.DMA((48,)),
+            pltpu.SemaphoreType.DMA((48,)),
+        ],
+        name="unpack",
+        compiler_params=pltpu.CompilerParams(vmem_limit_bytes=VMEM_BYTES),
+    )(total)
+    grads = grads[:-1] + (grads[-1].reshape(256),)
+    return (output, input_grad) + tuple(grads)
+
+
+VMEM_BYTES = 64 * 2**20 - 2**18
+
+
+ARG_SPECS = (P("dp", "seq", None), P("dp", None), P("dp"), P("dp", "seq", None)) + (P(),) * 20
+OUT_SPECS = (P("dp", "seq", None), P("dp", "seq", None)) + (P(),) * 20
+
+
 def solution(mesh):
+    shape = dict(mesh.shape)
+
+    def local(*args):
+        utterances, frames_in = args[0].shape[:2]
+        if fits(shape, utterances, frames_in):
+            return fused_local(shape, *args)
+        return general_local(*args)
+
     return jax.shard_map(
-        local,
-        mesh=mesh,
-        in_specs=(
-            P("dp", "seq", None),
-            P("dp", None),
-            P("dp"),
-            P("dp", "seq", None),
-            P(),
-            P(),
-            P(),
-            P(),
-            P(),
-            P(),
-            P(),
-            P(),
-            P(),
-            P(),
-            P(),
-            P(),
-            P(),
-            P(),
-            P(),
-            P(),
-            P(),
-            P(),
-            P(),
-            P(),
-        ),
-        out_specs=(
-            P("dp", "seq", None),
-            P("dp", "seq", None),
-            P(),
-            P(),
-            P(),
-            P(),
-            P(),
-            P(),
-            P(),
-            P(),
-            P(),
-            P(),
-            P(),
-            P(),
-            P(),
-            P(),
-            P(),
-            P(),
-            P(),
-            P(),
-            P(),
-            P(),
-        ),
-        check_vma=False,
-    )
+        local, mesh=mesh, in_specs=ARG_SPECS, out_specs=OUT_SPECS, check_vma=False
+    )

time: 1200 us -> 246 us (0.20); the launches traced: 1180 us -> 245 us
  matrix products: 358 us -> 0 us
  waiting for transfers between devices: 327 us -> 0 us
  Pallas kernels: 0 us -> 241 us
  local copies, waits for them, and re-layouts: 225 us -> 4.15 us
  blocking collectives: 124 us -> 0 us
  other arithmetic: 99 us -> 0 us
  starting transfers between devices: 33.1 us -> 0 us
  between operations: 18.1 us -> 0.69 us
    dot_general x91 -> x0, matrix products: 358 us -> none  [the longest x6 90.9 us: attend_out(): jnp.einsum('ufe,ec->ufc', snake_out, down_weight, precision=precise)]
    pallas_call x0 -> x2, Pallas kernels: none -> 241 us  [the longest x1 231 us: fused_local(): pl.pallas_call(lambda *refs: fused_kernel(shape, groups, *refs), out_shap...]
    psum x1 -> x0, waiting for transfers between devices: 202 us -> none  [local(): lax.psum(jnp.concatenate([flatten_all(grads_top), low_flat]), ('dp', 'seq'))]
    psum x8 -> x0, blocking collectives: 124 us -> none  [the longest x4 62.9 us: group_total(): return lax.psum((first_sum, second_sum), 'seq')]
    all_gather x4 -> x0, waiting for transfers between devices: 96.4 us -> none  [the longest x2 60.6 us: block_forward(): lax.all_gather(key_here, 'seq', axis=1, tiled=True)]
    unnamed x606 -> x2, local copies, waits for them, and re-layouts: 90.1 us -> 4.15 us
    reduce_sum x34 -> x0, other arithmetic: 46.1 us -> none  [the longest x2 14.4 us: attend_out(): scores = scores - jnp.max(scores, axis=3, keepdims=True)]
    slice x35 -> x0, local copies, waits for them, and re-layouts: 35.7 us -> none  [the longest x8 14.8 us: unflatten_all(): pieces.append(flat[offset_at:offset_at + size_in].reshape(shape_in))]
  transfers between devices with their start and end apart: 27 -> 0, of which waited for: 9 -> 0; matrix products, arithmetic and copies ran while one was open for 26% -> 0% of each run, Pallas kernels for 0% -> 0%
where the time goes in v1:
time: 246 us; the launch traced here: 245 us
  Pallas kernels  241 us (98%)
  local copies, waits for them, and re-layouts  4.15 us (2%)
    pallas_call x1, Pallas kernels, fused_local(): pl.pallas_call(lambda *refs: fused_kernel(shape, groups, *refs), out_shap...  231 us
    pallas_call x1, Pallas kernels, fused_local(): pl.pallas_call(lambda *refs: unpack_kernel(shape, *refs), out_shape=tuple...  9.28 us

profile of v1, /device:TPU:0, one launch (start us, length us, event | category | flops | bytes accessed | tf_op | source)
XLA Modules:
  0.0 245.4 jit_solution(13992613632817226028)
XLA Ops:
  0.7 231.3 %layers.1 = (f32[4,128,256]{2,1,0:T(8,128)}, f32[4,256,256]{2,1,0:T(8,128)}, f32[9984,256]{1,0:T(8,128)}) custom-call(f32[4,256,256]{2,1,0:T(8,128)} %refs_0_.1, f32[4,1024]{1,0:T(4,128)} %refs_1_.1, s32[4]{0:T(128)} %refs_2_.1, f32[4,128,256]{2,1,0:T(8,128)} %refs_3_.1, bf16[2,3,256,256]{3,2,1,0:T(8,128)(2,1)} %refs_4_.1, bf16[2,3,256,256]{3,2,1,0:T(8,128)(2,1)} %refs_5_.1, ...), custom_call_target="tpu_custom_call" | custom-call | tf_op jit(solution)/shard_map/layers/pallas_call | solution.py:2054
  232.0 9.3 %unpack.1 = (f32[2,3,256,256]{3,2,1,0:T(8,128)}, f32[2,3,256,256]{3,2,1,0:T(8,128)}, f32[2,256,256]{2,1,0:T(8,128)}, f32[2,2,256]{2,1,0:T(2,128)}, f32[2,2,256]{...) custom-call(f32[9984,256]{1,0:T(8,128)} %get-tuple-element.47.refs_0_), custom_call_target="tpu_custom_call" | custom-call | tf_op jit(solution)/shard_map/unpack/pallas_call | solution.py:2070
  241.3 1.9 copy.48
  243.2 2.3 copy.49
